TPU v7x, 512 devices: a whole 4x8x8 slice. The times are simulated.
512 devices in a mesh: dom: 64 (over z_lo, x, y), rep: 8 (over z_hi, core).
Axes of the slice: x: 4, y: 8, z: 8 (z_hi: 4, z_lo: 2; z = z_hi * 2 + z_lo), core: 2. Of those that a mesh axis runs over, the one named last changes fastest.
Arguments:
- features: bfloat16 [32768, 256], P('dom'), may hold values from -6 to 6
- weight: bfloat16 [256, 256], replicated, may hold values from -0.375 to 0.375
- grad_out: bfloat16 [32768, 256], P('dom'), may hold values from -6 to 6
- tiles: bfloat16 [64, 64, 512, 512], P('dom', 'rep'), may hold values from -0.125 to 0.125
- tile_mask: int32 [64, 64], P('dom', 'rep'), may hold values from 0 to 1, as said below
Outputs:
- activated: bfloat16 [32768, 256], P('dom')
- feature_grad: bfloat16 [32768, 256], P('dom')
- weight_grad: float32 [256, 256], replicated
Inputs may be any that keep to these rules, and one draw needn't show every extreme that they name: `tile_mask`: the diagonal tiles (offset 0) are always present; other tiles are sparse, more frequent near the diagonal (small offsets or offsets near 64), and some row blocks hold many more tiles than others.
All inputs are finite; a program needn't handle non-finite values.
Results may differ from a plain program's by a relative error of at most 0.007.
Values may be sent and summed in bfloat16 or wider, within the bound.
No kernel may reach another device: no remote copies, remote signals or barrier semaphores. Data moves between devices by JAX's collectives and lax.ppermute only.
A program may use at most 64 MiB of HBM per device.

v0:
```python
import jax
import jax.numpy as jnp
from jax import lax
from jax.sharding import PartitionSpec as P


def shifted_2(block, axis, distance):
    devices = range(lax.axis_size(axis))
    route = [((i - distance) % len(devices), i) for i in devices]
    return lax.ppermute(block, axis, route)


def tile_product(tile, weight_flag, operand, transposed):
    if transposed:
        contraction = (((0,), (0,)), ((), ()))
        out_rows = tile.shape[1]
    else:
        contraction = (((1,), (0,)), ((), ()))
        out_rows = tile.shape[0]

    def compute():
        return lax.dot_general(tile, operand, contraction, preferred_element_type=jnp.float32)

    def skipped():
        return jnp.zeros((out_rows, operand.shape[1]), jnp.float32)

    return lax.cond(weight_flag > 0, compute, skipped)


def shards(features, weight, grad_out, tiles, tile_mask):
    domains = lax.axis_size("dom")
    replicas = lax.axis_size("rep")
    sections = domains // replicas
    replica = lax.axis_index("rep")
    bit_count = replicas.bit_length() - 1
    rows_here = features.shape[0]
    hidden = features.shape[1]
    projected = jnp.dot(features, weight, preferred_element_type=jnp.float32).astype(jnp.bfloat16)
    current = projected
    for level in range(bit_count):
        shifted = shifted_2(current, "dom", sections << level)
        current = jnp.where(replica >> level & 1 == 1, shifted, current)
    partial_value = jnp.zeros((rows_here, hidden), jnp.float32)
    for section in range(sections):
        if section > 0:
            current = shifted_2(current, "dom", 1)
        partial_value = partial_value + tile_product(
            tiles[0, section], tile_mask[0, section], current, False
        )
    total = lax.psum(partial_value, "rep")
    gate_value = jax.nn.sigmoid(total)
    activated = (total * gate_value).astype(jnp.bfloat16)
    score_grad = (
        grad_out.astype(jnp.float32) * gate_value * (1.0 + total * (1.0 - gate_value))
    ).astype(jnp.bfloat16)
    carried = tile_product(tiles[0, sections - 1], tile_mask[0, sections - 1], score_grad, True)
    for section in range(sections - 2, -1, -1):
        carried = shifted_2(carried, "dom", -1)
        carried = carried + tile_product(tiles[0, section], tile_mask[0, section], score_grad, True)
    for level in range(bit_count):
        shifted = shifted_2(carried, "dom", -(sections << level))
        carried = jnp.where(replica >> level & 1 == 1, shifted, carried)
    node_grad = lax.psum(carried, "rep").astype(jnp.bfloat16)
    feature_grad = lax.dot_general(
        node_grad, weight, (((1,), (1,)), ((), ())), preferred_element_type=jnp.float32
    ).astype(jnp.bfloat16)
    scaling = (rows_here * domains) ** (-0.5)
    weight_term = lax.dot_general(
        features, node_grad, (((0,), (0,)), ((), ())), preferred_element_type=jnp.float32
    )
    weight_grad = lax.psum(weight_term, "dom") * scaling
    return (activated, feature_grad, weight_grad)


def solution(mesh):
    placed = (P("dom", None), P(), P("dom", None), P("dom", "rep", None, None), P("dom", "rep"))
    return jax.shard_map(
        shards,
        mesh=mesh,
        in_specs=placed,
        out_specs=(P("dom", None), P("dom", None), P()),
        check_vma=False,
    )
```

profile of v0, /device:TPU:64, one launch (start us, length us, event | category | flops | bytes accessed | tf_op | source)
XLA Modules:
  0.0 1001.3 jit_solution(10633392570459055978)
XLA Ops:
  7.2 0.9 copy-done
  8.1 1.1 convolution_convert_fusion.1
  9.2 3.4 collective-permute-start
  12.7 8.6 collective-permute-done
  21.3 2.8 collective-permute-start.1
  24.2 8.6 collective-permute-done.1
  32.8 4.6 collective-permute-start.2
  37.5 4.3 collective-permute-done.2
  41.9 2.8 collective-permute-start.3
  44.6 9.7 collective-permute-done.3
  54.3 1.9 collective-permute-start.4
  56.3 10.5 %collective-permute-done.4 = bf16[512,256]{1,0:T(8,128)(2,1)S(1)} collective-permute-done((bf16[512,256]{1,0:T(8,128)(2,1)S(1)}, bf16[512,256]{1,0:T(8,128)(2,1)S(1)}, u32[]{:S(2)}, u32[]{:S(2)}) %collective-permute-start.4) | collective-permute-done | bytes 262176 | tf_op jit(solution)/shard_map/ppermute | solution.py:10
  66.8 1.9 collective-permute-start.5
  68.7 10.5 %collective-permute-done.5 = bf16[512,256]{1,0:T(8,128)(2,1)S(1)} collective-permute-done((bf16[512,256]{1,0:T(8,128)(2,1)S(1)}, bf16[512,256]{1,0:T(8,128)(2,1)S(1)}, u32[]{:S(2)}, u32[]{:S(2)}) %collective-permute-start.5) | collective-permute-done | bytes 262176 | tf_op jit(solution)/shard_map/ppermute | solution.py:10
  79.3 1.9 collective-permute-start.6
  81.2 10.5 %collective-permute-done.6 = bf16[512,256]{1,0:T(8,128)(2,1)S(1)} collective-permute-done((bf16[512,256]{1,0:T(8,128)(2,1)S(1)}, bf16[512,256]{1,0:T(8,128)(2,1)S(1)}, u32[]{:S(2)}, u32[]{:S(2)}) %collective-permute-start.6) | collective-permute-done | bytes 262176 | tf_op jit(solution)/shard_map/ppermute | solution.py:10
  91.8 1.9 collective-permute-start.7
  93.7 11.4 %collective-permute-done.7 = bf16[512,256]{1,0:T(8,128)(2,1)S(1)} collective-permute-done((bf16[512,256]{1,0:T(8,128)(2,1)S(1)}, bf16[512,256]{1,0:T(8,128)(2,1)S(1)}, u32[]{:S(2)}, u32[]{:S(2)}) %collective-permute-start.7) | collective-permute-done | bytes 262176 | tf_op jit(solution)/shard_map/ppermute | solution.py:10
  105.0 1.9 collective-permute-start.8
  107.0 1.6 fusion.2
  113.8 5.4 collective-permute-done.8
  119.2 1.9 collective-permute-start.9
  121.1 3.6 slice_bitcast_fusion.6
  124.7 2.2 conditional.16
  124.7 2.2 fusion.3
  127.0 2.1 conditional.17
  127.0 2.1 fusion.4
  132.4 0.9 conditional.23
  133.3 3.1 add_add_fusion
  136.4 82.6 %all-reduce.4.cloned.1.call-done = f32[512,256]{1,0:T(8,128)} async-done(((f32[512,256]{1,0:T(8,128)}), f32[512,256]{1,0:T(8,128)}) %all-reduce.4.cloned.1.call-update) | async-done | bytes 524304 | tf_op jit(solution)/shard_map/psum | solution.py:50
  219.0 2.0 multiply_convert_fusion
  221.9 7.6 collective-permute-start.10
  230.4 10.9 %collective-permute-done.10 = f32[512,256]{1,0:T(8,128)} collective-permute-done((f32[512,256]{1,0:T(8,128)}, f32[512,256]{1,0:T(8,128)}, u32[]{:S(2)}, u32[]{:S(2)}) %collective-permute-start.10) | collective-permute-done | bytes 524320 | tf_op jit(solution)/shard_map/ppermute | solution.py:10
  241.3 2.1 add.63
  243.4 8.6 collective-permute-start.11
  252.0 0.9 conditional.26
  252.9 10.0 %collective-permute-done.11 = f32[512,256]{1,0:T(8,128)} collective-permute-done((f32[512,256]{1,0:T(8,128)}, f32[512,256]{1,0:T(8,128)}, u32[]{:S(2)}, u32[]{:S(2)}) %collective-permute-start.11) | collective-permute-done | bytes 524320 | tf_op jit(solution)/shard_map/ppermute | solution.py:10
  262.9 2.1 add.64
  265.0 8.6 collective-permute-start.12
  273.6 0.8 conditional.27
  274.4 9.1 collective-permute-done.12
  283.6 2.1 add.65
  285.7 8.6 collective-permute-start.13
  294.3 9.0 collective-permute-done.13
  303.3 1.9 add.66
  305.2 8.6 collective-permute-start.14
  313.9 8.1 collective-permute-done.14
  322.0 1.1 add.67
  323.1 8.6 collective-permute-start.15
  332.1 6.5 collective-permute-done.15
  338.6 1.1 add.68
  339.7 8.7 collective-permute-start.16
  348.8 6.3 collective-permute-done.16
  355.2 1.9 collective-permute-start.17
  357.1 11.1 %collective-permute-done.17 = f32[512,256]{1,0:T(8,128)S(1)} collective-permute-done((f32[512,256]{1,0:T(8,128)S(1)}, f32[512,256]{1,0:T(8,128)S(1)}, u32[]{:S(2)}, u32[]{:S(2)}) %collective-permute-start.17) | collective-permute-done | bytes 524320 | tf_op jit(solution)/shard_map/ppermute | solution.py:10
  368.3 1.9 collective-permute-start.18
  370.2 11.7 %collective-permute-done.18 = f32[512,256]{1,0:T(8,128)S(1)} collective-permute-done((f32[512,256]{1,0:T(8,128)S(1)}, f32[512,256]{1,0:T(8,128)S(1)}, u32[]{:S(2)}, u32[]{:S(2)}) %collective-permute-start.18) | collective-permute-done | bytes 524320 | tf_op jit(solution)/shard_map/ppermute | solution.py:10
  382.0 1.9 collective-permute-start.19
  383.9 9.3 collective-permute-done.19
  393.3 46.7 %all-reduce.7 = bf16[512,256]{1,0:T(8,128)(2,1)S(1)} all-reduce(f32[512,256]{1,0:T(8,128)S(1)} %broadcast_select_fusion.4), channel_id=1, replica_groups=mesh['dom'=64,'rep'=8] {'rep'}, use_global_device_ids=true, to_apply=%region_33.34 | all-reduce | flops 131072 | bytes 786432 | tf_op jit(solution)/shard_map/psum | solution.py:63
  440.0 1.0 convolution_bitcast_fusion
  441.0 1.0 convolution_convert_fusion
  442.0 550.7 %all-reduce.6.cloned.1.call-done = f32[256,256]{0,1:T(8,128)} async-done(((f32[256,256]{0,1:T(8,128)}), f32[256,256]{0,1:T(8,128)}) %all-reduce.6.cloned.1.call-update) | async-done | bytes 262160 | tf_op jit(solution)/shard_map/psum | solution.py:71
  992.7 1.0 broadcast_multiply_fusion
  (55 shorter events, 15.6 us)
Async XLA Ops:
  7.2 1.0 copy-start
  7.2 211.9 %all-reduce.4.cloned.1.call-start = ((), (), s32[]{:S(2)}) async-start(), calls=%async_computation | async-start | bytes 1048576 | tf_op jit(solution)/shard_map/psum | solution.py:50
  9.2 12.0 %collective-permute-start = (bf16[512,256]{1,0:T(8,128)(2,1)S(1)}, bf16[512,256]{1,0:T(8,128)(2,1)S(1)}, u32[]{:S(2)}, u32[]{:S(2)}) collective-permute-start(bf16[512,256]{1,0:T(8,128)(2,1)S(1)} %convolution_convert_fusion.1), channel_id=1, source_target_pairs={{448,0},{456,8},{464,16},{472,24},{480,32},{488,40},{496,48},{504,... | collective-permute-start | bytes 786440 | tf_op jit(solution)/shard_map/ppermute | solution.py:10
  21.3 11.5 %collective-permute-start.1 = (bf16[512,256]{1,0:T(8,128)(2,1)S(1)}, bf16[512,256]{1,0:T(8,128)(2,1)S(1)}, u32[]{:S(2)}, u32[]{:S(2)}) collective-permute-start(bf16[512,256]{1,0:T(8,128)(2,1)S(1)} %broadcast_select_fusion.1), channel_id=1, source_target_pairs={{384,0},{392,8},{400,16},{408,24},{416,32},{424,40},{432,48},{440,... | collective-permute-start | bytes 786440 | tf_op jit(solution)/shard_map/ppermute | solution.py:10
  32.8 9.0 collective-permute-start.2
  41.8 77.4 %copy-start.2 = (bf16[512,256]{1,0:T(8,128)(2,1)}, bf16[512,256]{1,0:T(8,128)(2,1)S(1)}, u32[]{:S(2)}) copy-start(bf16[512,256]{1,0:T(8,128)(2,1)S(1)} %broadcast_select_fusion.5) | copy-start | bytes 786436
  41.9 12.5 %collective-permute-start.3 = (bf16[512,256]{1,0:T(8,128)(2,1)S(1)}, bf16[512,256]{1,0:T(8,128)(2,1)S(1)}, u32[]{:S(2)}, u32[]{:S(2)}) collective-permute-start(bf16[512,256]{1,0:T(8,128)(2,1)S(1)} %broadcast_select_fusion.5), channel_id=1, source_target_pairs={{504,0},{0,8},{8,16},{16,24},{24,32},{32,40},{40,48},{48,56},{56,6... | collective-permute-start | bytes 786440 | tf_op jit(solution)/shard_map/ppermute | solution.py:10
  54.3 1.9 copy-start.8
  54.3 12.5 %collective-permute-start.4 = (bf16[512,256]{1,0:T(8,128)(2,1)S(1)}, bf16[512,256]{1,0:T(8,128)(2,1)S(1)}, u32[]{:S(2)}, u32[]{:S(2)}) collective-permute-start(bf16[512,256]{1,0:T(8,128)(2,1)S(1)} %collective-permute-done.3), channel_id=1, source_target_pairs={{504,0},{0,8},{8,16},{16,24},{24,32},{32,40},{40,48},{48,56},{56,6... | collective-permute-start | bytes 786440 | tf_op jit(solution)/shard_map/ppermute | solution.py:10
  66.8 1.9 copy-start.7
  66.8 12.5 %collective-permute-start.5 = (bf16[512,256]{1,0:T(8,128)(2,1)S(1)}, bf16[512,256]{1,0:T(8,128)(2,1)S(1)}, u32[]{:S(2)}, u32[]{:S(2)}) collective-permute-start(bf16[512,256]{1,0:T(8,128)(2,1)S(1)} %collective-permute-done.4), channel_id=1, source_target_pairs={{504,0},{0,8},{8,16},{16,24},{24,32},{32,40},{40,48},{48,56},{56,6... | collective-permute-start | bytes 786440 | tf_op jit(solution)/shard_map/ppermute | solution.py:10
  79.3 1.9 copy-start.6
  79.3 12.5 %collective-permute-start.6 = (bf16[512,256]{1,0:T(8,128)(2,1)S(1)}, bf16[512,256]{1,0:T(8,128)(2,1)S(1)}, u32[]{:S(2)}, u32[]{:S(2)}) collective-permute-start(bf16[512,256]{1,0:T(8,128)(2,1)S(1)} %collective-permute-done.5), channel_id=1, source_target_pairs={{504,0},{0,8},{8,16},{16,24},{24,32},{32,40},{40,48},{48,56},{56,6... | collective-permute-start | bytes 786440 | tf_op jit(solution)/shard_map/ppermute | solution.py:10
  91.8 27.4 %copy-start.5 = (bf16[512,256]{1,0:T(8,128)(2,1)}, bf16[512,256]{1,0:T(8,128)(2,1)S(1)}, u32[]{:S(2)}) copy-start(bf16[512,256]{1,0:T(8,128)(2,1)S(1)} %collective-permute-done.6) | copy-start | bytes 786436
  91.8 13.3 %collective-permute-start.7 = (bf16[512,256]{1,0:T(8,128)(2,1)S(1)}, bf16[512,256]{1,0:T(8,128)(2,1)S(1)}, u32[]{:S(2)}, u32[]{:S(2)}) collective-permute-start(bf16[512,256]{1,0:T(8,128)(2,1)S(1)} %collective-permute-done.6), channel_id=1, source_target_pairs={{504,0},{0,8},{8,16},{16,24},{24,32},{32,40},{40,48},{48,56},{56,6... | collective-permute-start | bytes 786440 | tf_op jit(solution)/shard_map/ppermute | solution.py:10
  105.0 14.2 %copy-start.4 = (bf16[512,256]{1,0:T(8,128)(2,1)}, bf16[512,256]{1,0:T(8,128)(2,1)S(1)}, u32[]{:S(2)}) copy-start(bf16[512,256]{1,0:T(8,128)(2,1)S(1)} %collective-permute-done.7) | copy-start | bytes 786436
  105.0 14.2 %collective-permute-start.8 = (bf16[512,256]{1,0:T(8,128)(2,1)S(1)}, bf16[512,256]{1,0:T(8,128)(2,1)}, u32[]{:S(2)}, u32[]{:S(2)}) collective-permute-start(bf16[512,256]{1,0:T(8,128)(2,1)S(1)} %collective-permute-done.7), channel_id=1, source_target_pairs={{504,0},{0,8},{8,16},{16,24},{24,32},{32,40},{40,48},{48,56},{56,6... | collective-permute-start | bytes 786440 | tf_op jit(solution)/shard_map/ppermute | solution.py:10
  119.2 13.2 %collective-permute-start.9 = (bf16[512,256]{1,0:T(8,128)(2,1)}, bf16[512,256]{1,0:T(8,128)(2,1)}, u32[]{:S(2)}, u32[]{:S(2)}) collective-permute-start(bf16[512,256]{1,0:T(8,128)(2,1)} %collective-permute-done.8), channel_id=1, source_target_pairs={{504,0},{0,8},{8,16},{16,24},{24,32},{32,40},{40,48},{48,56},{56,6... | collective-permute-start | bytes 786440 | tf_op jit(solution)/shard_map/ppermute | solution.py:10
  124.7 6.8 copy-start.1
  136.4 856.3 %all-reduce.6.cloned.1.call-start = ((), (), s32[]{:S(2)}) async-start(), calls=%async_computation.1 | async-start | bytes 524288 | tf_op jit(solution)/shard_map/psum | solution.py:71
  221.9 19.4 %collective-permute-start.10 = (f32[512,256]{1,0:T(8,128)}, f32[512,256]{1,0:T(8,128)}, u32[]{:S(2)}, u32[]{:S(2)}) collective-permute-start(f32[512,256]{1,0:T(8,128)} %get-tuple-element.176), channel_id=1, source_target_pairs={{8,0},{16,8},{24,16},{32,24},{40,32},{48,40},{56,48},{64,56},{72,6... | collective-permute-start | bytes 1572872 | tf_op jit(solution)/shard_map/ppermute | solution.py:10
  243.4 19.5 %collective-permute-start.11 = (f32[512,256]{1,0:T(8,128)}, f32[512,256]{1,0:T(8,128)}, u32[]{:S(2)}, u32[]{:S(2)}) collective-permute-start(f32[512,256]{1,0:T(8,128)} %add.63), channel_id=1, source_target_pairs={{8,0},{16,8},{24,16},{32,24},{40,32},{48,40},{56,48},{64,56},{72,6... | collective-permute-start | bytes 1572872 | tf_op jit(solution)/shard_map/ppermute | solution.py:10
  265.0 18.6 %collective-permute-start.12 = (f32[512,256]{1,0:T(8,128)}, f32[512,256]{1,0:T(8,128)}, u32[]{:S(2)}, u32[]{:S(2)}) collective-permute-start(f32[512,256]{1,0:T(8,128)} %add.64), channel_id=1, source_target_pairs={{8,0},{16,8},{24,16},{32,24},{40,32},{48,40},{56,48},{64,56},{72,6... | collective-permute-start | bytes 1572872 | tf_op jit(solution)/shard_map/ppermute | solution.py:10
  285.7 17.7 %collective-permute-start.13 = (f32[512,256]{1,0:T(8,128)}, f32[512,256]{1,0:T(8,128)}, u32[]{:S(2)}, u32[]{:S(2)}) collective-permute-start(f32[512,256]{1,0:T(8,128)} %add.65), channel_id=1, source_target_pairs={{8,0},{16,8},{24,16},{32,24},{40,32},{48,40},{56,48},{64,56},{72,6... | collective-permute-start | bytes 1572872 | tf_op jit(solution)/shard_map/ppermute | solution.py:10
  305.2 16.7 %collective-permute-start.14 = (f32[512,256]{1,0:T(8,128)}, f32[512,256]{1,0:T(8,128)}, u32[]{:S(2)}, u32[]{:S(2)}) collective-permute-start(f32[512,256]{1,0:T(8,128)} %add.66), channel_id=1, source_target_pairs={{8,0},{16,8},{24,16},{32,24},{40,32},{48,40},{56,48},{64,56},{72,6... | collective-permute-start | bytes 1572872 | tf_op jit(solution)/shard_map/ppermute | solution.py:10
  323.1 15.5 %collective-permute-start.15 = (f32[512,256]{1,0:T(8,128)S(1)}, f32[512,256]{1,0:T(8,128)}, u32[]{:S(2)}, u32[]{:S(2)}) collective-permute-start(f32[512,256]{1,0:T(8,128)S(1)} %add.67), channel_id=1, source_target_pairs={{8,0},{16,8},{24,16},{32,24},{40,32},{48,40},{56,48},{64,56},{72,6... | collective-permute-start | bytes 1572872 | tf_op jit(solution)/shard_map/ppermute | solution.py:10
  339.7 15.4 %collective-permute-start.16 = (f32[512,256]{1,0:T(8,128)S(1)}, f32[512,256]{1,0:T(8,128)S(1)}, u32[]{:S(2)}, u32[]{:S(2)}) collective-permute-start(f32[512,256]{1,0:T(8,128)S(1)} %add.68), channel_id=1, source_target_pairs={{8,0},{16,8},{24,16},{32,24},{40,32},{48,40},{56,48},{64,56},{72,6... | collective-permute-start | bytes 1572872 | tf_op jit(solution)/shard_map/ppermute | solution.py:10
  348.8 92.2 %copy-start.3 = (bf16[256,256]{1,0:T(8,128)(2,1)S(1)}, bf16[256,256]{1,0:T(8,128)(2,1)}, u32[]{:S(2)}) copy-start(bf16[256,256]{1,0:T(8,128)(2,1)} %param.38) | copy-start | bytes 393220
  355.2 13.0 %collective-permute-start.17 = (f32[512,256]{1,0:T(8,128)S(1)}, f32[512,256]{1,0:T(8,128)S(1)}, u32[]{:S(2)}, u32[]{:S(2)}) collective-permute-start(f32[512,256]{1,0:T(8,128)S(1)} %add.69), channel_id=1, source_target_pairs={{64,0},{72,8},{80,16},{88,24},{96,32},{104,40},{112,48},{120,56},{... | collective-permute-start | bytes 1572872 | tf_op jit(solution)/shard_map/ppermute | solution.py:10
  368.3 13.6 %collective-permute-start.18 = (f32[512,256]{1,0:T(8,128)S(1)}, f32[512,256]{1,0:T(8,128)S(1)}, u32[]{:S(2)}, u32[]{:S(2)}) collective-permute-start(f32[512,256]{1,0:T(8,128)S(1)} %broadcast_select_fusion), channel_id=1, source_target_pairs={{128,0},{136,8},{144,16},{152,24},{160,32},{168,40},{176,48},{184,... | collective-permute-start | bytes 1572872 | tf_op jit(solution)/shard_map/ppermute | solution.py:10
  382.0 11.2 %collective-permute-start.19 = (f32[512,256]{1,0:T(8,128)S(1)}, f32[512,256]{1,0:T(8,128)S(1)}, u32[]{:S(2)}, u32[]{:S(2)}) collective-permute-start(f32[512,256]{1,0:T(8,128)S(1)} %broadcast_select_fusion.2), channel_id=1, source_target_pairs={{256,0},{264,8},{272,16},{280,24},{288,32},{296,40},{304,48},{312,... | collective-permute-start | bytes 1572872 | tf_op jit(solution)/shard_map/ppermute | solution.py:10
Sparse Core Ops, SparseCore 0:
  136.5 82.5 all-reduce.3
  441.1 551.5 all-reduce.5
where the time goes:
time: 1000 us
  waiting for transfers between devices  805 us (80%)
  starting transfers between devices  90.3 us (9%)
  blocking collectives  46.7 us (5%)
  between operations  19.6 us (2%)
  other arithmetic  16.8 us (2%)
  local copies, waits for them, and re-layouts  14.7 us (1%)
    psum x1, waiting for transfers between devices, shards(): weight_grad = lax.psum(weight_term, 'dom') * scaling  551 us
    ppermute x20, waiting for transfers between devices, shifted_2(): return lax.ppermute(block, axis, route)  172 us
    ppermute x20, starting transfers between devices, shifted_2(): return lax.ppermute(block, axis, route)  90.2 us
    psum x1, waiting for transfers between devices, shards(): total = lax.psum(partial_value, 'rep')  82.6 us
    psum x1, blocking collectives, shards(): node_grad = lax.psum(carried, 'rep').astype(jnp.bfloat16)  46.7 us
  transfers between devices with their start and end apart: 22, of which 21 were waited for; matrix products, arithmetic and copies ran while one was open for 2% of the time, Pallas kernels for 0%

commit v1 on v0

v1 whole, which is shorter than its diff:
```python
import functools

import jax
import jax.numpy as jnp
from jax import lax
from jax.experimental import pallas as pl
from jax.experimental.pallas import tpu as pltpu
from jax.sharding import Mesh
from jax.sharding import PartitionSpec as P

AXES = ("zl", "x", "y", "zh", "c")
SIZES = (2, 4, 8, 4, 2)
DOM = ("zl", "x", "y")
BLOCKS = 64
REPLICAS = 8
ROWS = 512
HALF = 256
HIDDEN = 256
F32 = jnp.float32
BF16 = jnp.bfloat16
SMEM = pl.BlockSpec(memory_space=pltpu.SMEM)
VMEM = pl.BlockSpec(memory_space=pltpu.VMEM)
ANY = pl.BlockSpec(memory_space=pl.ANY)
PARAMS = pltpu.CompilerParams(vmem_limit_bytes=40 * 1024 * 1024)


def route(value, target):
    pairs = []
    for i in range(BLOCKS):
        for r in range(REPLICAS):
            i2, r2 = target(i, r)
            pairs.append((i * REPLICAS + r, (i2 % BLOCKS) * REPLICAS + r2 % REPLICAS))
    return lax.ppermute(value, AXES, pairs)


def first_of(r):
    return 4 * (r % 2)


def partner(i, r):
    return (i + 8, r + 1) if r % 2 == 0 else (i - 8, r - 1)


def swap_pair(value):
    return route(value, partner)


def swap_core(value):
    return lax.ppermute(value, "c", [(0, 1), (1, 0)])


def start_tiles(mask_ref, tiles_ref, held, sems, indices):
    for t in indices:

        @pl.when(mask_ref[0, t] > 0)
        def _():
            pltpu.make_async_copy(tiles_ref.at[0, t], held.at[t], sems.at[t]).start()


def wait_tile(tiles_ref, held, sems, t):
    pltpu.make_async_copy(tiles_ref.at[0, t], held.at[t], sems.at[t]).wait()


def forward_kernel(core_ref, mask_ref, tiles_ref, g0, g1, g2, g3, e12, e03, keep_ref, send_ref, held, acc, sems):
    core = core_ref[0]
    mine, other = core * 4, 4 - core * 4
    order = [
        (mine + 1, g1, 0),
        (mine + 2, g2, 0),
        (mine, g0, 0),
        (mine + 3, g3, 0),
        (other + 1, e12, 0),
        (other + 2, e12, ROWS),
        (other, e03, 0),
        (other + 3, e03, ROWS),
    ]
    start_tiles(mask_ref, tiles_ref, held, sems, [t for t, _, _ in order])
    acc[...] = jnp.zeros_like(acc)
    for t, block, start in order:

        @pl.when(mask_ref[0, t] > 0)
        def _():
            wait_tile(tiles_ref, held, sems, t)
            acc[...] += jnp.dot(held[t], block[start : start + ROWS, :], preferred_element_type=F32)

    keep_ref[...] = acc[pl.ds(pl.multiple_of(core * HALF, HALF), HALF), :]
    send_ref[...] = acc[pl.ds(pl.multiple_of(HALF - core * HALF, HALF), HALF), :]


def middle_kernel(zh_ref, parts_ref, weight_ref, grad_ref, pack_ref, term_ref, full):
    wide = parts_ref[0].astype(F32)
    for s in range(1, 4):
        wide = wide + parts_ref[s].astype(F32)
    high = wide.astype(BF16)
    low = (wide - high.astype(F32)).astype(BF16)
    weight = weight_ref[...]
    total = jnp.dot(high, weight, preferred_element_type=F32) + jnp.dot(low, weight, preferred_element_type=F32)
    gate = jax.nn.sigmoid(total)
    pack_ref[0] = (total * gate).astype(BF16)
    score = (grad_ref[...].astype(F32) * gate * (1.0 + total * (1.0 - gate))).astype(BF16)
    pack_ref[1] = lax.dot_general(weight, score, (((1,), (1,)), ((), ())), preferred_element_type=F32).astype(BF16)
    full[...] = lax.dot_general(high, score, (((0,), (0,)), ((), ())), preferred_element_type=F32)
    term_ref[...] = full[pl.ds(pl.multiple_of(zh_ref[0] * 64, 64), 64), :]


def backward_kernel(plan, core_ref, mask_ref, tiles_ref, pack_ref, *rest):
    outs, held, sems = rest[: len(plan)], rest[-2], rest[-1]
    core = core_ref[0]
    base = (core * 4, 4 - core * 4)
    work = [(base[side] + q, out, slot) for out, entries in zip(outs, plan) for slot, (side, q) in enumerate(entries)]
    start_tiles(mask_ref, tiles_ref, held, sems, [t for t, _, _ in work])
    for t, out, slot in work:

        @pl.when(mask_ref[0, t] > 0)
        def _():
            wait_tile(tiles_ref, held, sems, t)
            value = jnp.dot(pack_ref[0, 1], held[t, :HALF, :], preferred_element_type=F32)
            value = value + jnp.dot(pack_ref[1, 1], held[t, HALF:, :], preferred_element_type=F32)
            value = value.astype(BF16)
            out[slot, 0] = value[:, :HALF]
            out[slot, 1] = value[:, HALF:]

        @pl.when(mask_ref[0, t] == 0)
        def _():
            out[slot] = jnp.zeros((2, HIDDEN, HALF), BF16)


def last_kernel(parts_ref, out_ref):
    wide = parts_ref[0].astype(F32)
    for s in range(1, 4):
        wide = wide + parts_ref[s].astype(F32)
    out_ref[...] = wide.T.astype(BF16)


def products(plan, core, mask, tiles, pack):
    return pl.pallas_call(
        functools.partial(backward_kernel, plan),
        out_shape=[jax.ShapeDtypeStruct((len(entries), 2, HIDDEN, HALF), BF16) for entries in plan],
        in_specs=[SMEM, SMEM, ANY, VMEM],
        out_specs=[VMEM] * len(plan),
        scratch_shapes=[pltpu.VMEM((8, ROWS, ROWS), BF16), pltpu.SemaphoreType.DMA((8,))],
        compiler_params=PARAMS,
        cost_estimate=pl.CostEstimate(flops=10**9, bytes_accessed=6 * 2**20, transcendentals=0),
    )(core, mask, tiles, pack)


def total_of(*values):
    wide = values[0].astype(F32)
    for value in values[1:]:
        wide = wide + value.astype(F32)
    return wide


def shards(features, weight, grad_out, tiles, tile_mask):
    core_index = lax.axis_index("c")
    core = core_index.astype(jnp.int32).reshape(1)
    zh = lax.axis_index("zh").astype(jnp.int32).reshape(1)

    g1 = route(features, lambda i, r: (i + 8 * r + first_of(r) + 1, r))
    g2 = route(features, lambda i, r: (i + 8 * r + first_of(r) + 2, r))
    g0 = route(g1, lambda i, r: (i - 1, r))
    g3 = route(g2, lambda i, r: (i + 1, r))
    e12 = swap_pair(jnp.concatenate([g1, g2]))
    e03 = swap_pair(jnp.concatenate([g0, g3]))
    half = jax.ShapeDtypeStruct((HALF, HIDDEN), F32)
    keep, send = pl.pallas_call(
        forward_kernel,
        out_shape=[half, half],
        in_specs=[SMEM, SMEM, ANY] + [VMEM] * 6,
        out_specs=[VMEM, VMEM],
        scratch_shapes=[
            pltpu.VMEM((8, ROWS, ROWS), BF16),
            pltpu.VMEM((ROWS, HIDDEN), F32),
            pltpu.SemaphoreType.DMA((8,)),
        ],
        compiler_params=PARAMS,
        cost_estimate=pl.CostEstimate(flops=10**9, bytes_accessed=6 * 2**20, transcendentals=0),
    )(core, tile_mask, tiles, g0, g1, g2, g3, e12, e03)
    chip = (keep + swap_core(send)).astype(BF16)
    parts = lax.all_gather(chip, "zh")
    grad_half = lax.dynamic_slice_in_dim(grad_out, core_index * HALF, HALF, 0)
    pack, term = pl.pallas_call(
        middle_kernel,
        out_shape=[
            jax.ShapeDtypeStruct((2, HALF, HIDDEN), BF16),
            jax.ShapeDtypeStruct((64, HIDDEN), F32),
        ],
        in_specs=[SMEM] + [VMEM] * 3,
        out_specs=[VMEM, VMEM],
        scratch_shapes=[pltpu.VMEM((HIDDEN, HIDDEN), F32)],
        compiler_params=PARAMS,
    )(zh, parts, weight, grad_half)
    packs = lax.all_gather(pack, "c")
    activated = packs[:, 0].reshape(ROWS, HIDDEN)

    (send03,) = products((((1, 0), (1, 3)),), core, tile_mask, tiles, packs)
    r03 = swap_pair(send03)
    send12, own = products((((1, 1), (1, 2)), ((0, 0), (0, 1), (0, 2), (0, 3))), core, tile_mask, tiles, packs)
    r12 = swap_pair(send12)
    n0 = total_of(own[0], r03[0]).astype(BF16)
    n3 = total_of(own[3], r03[1]).astype(BF16)
    t0 = route(n0, lambda i, r: (i + 1, r))
    t3 = route(n3, lambda i, r: (i - 1, r))
    n1 = total_of(own[1], r12[0], t0).astype(BF16)
    n2 = total_of(own[2], r12[1], t3).astype(BF16)
    d1 = route(n1, lambda i, r: (i - 8 * r - first_of(r) - 1, r))
    d2 = route(n2, lambda i, r: (i - 8 * r - first_of(r) - 2, r))
    both = total_of(d1, d2)
    flipped = jnp.where(core_index == 0, both[1], both[0])
    kept = jnp.where(core_index == 0, both[0], both[1])
    chip_grad = (kept + swap_core(flipped)).astype(BF16)
    grad_parts = lax.all_gather(chip_grad, "zh")
    grad_rows = pl.pallas_call(
        last_kernel,
        out_shape=jax.ShapeDtypeStruct((HALF, HIDDEN), BF16),
        in_specs=[VMEM],
        out_specs=VMEM,
        compiler_params=PARAMS,
    )(grad_parts)
    feature_grad = lax.all_gather(grad_rows, "c").reshape(ROWS, HIDDEN)

    spread = lax.all_to_all(term.reshape(BLOCKS, 1, HIDDEN), DOM, 0, 0)
    row = jnp.sum(spread, axis=0)
    row = (row + swap_core(row)) * (BLOCKS * ROWS) ** -0.5
    rows = lax.all_to_all(jnp.broadcast_to(row, (256, 1, HIDDEN)), ("zh",) + DOM, 0, 0)
    return activated, feature_grad, rows.reshape(HIDDEN, HIDDEN)


def solution(mesh):
    fine = Mesh(mesh.devices.reshape(SIZES), AXES)
    nodes = P(DOM, None)
    return jax.shard_map(
        shards,
        mesh=fine,
        in_specs=(nodes, P(), nodes, P(DOM, ("zh", "c"), None, None), P(DOM, ("zh", "c"))),
        out_specs=(nodes, nodes, P()),
        check_vma=False,
    )
```

time: 1000 us -> 183 us (0.18)
  the two profiles are of different devices: /device:TPU:64 before, /device:TPU:1 now
where the time goes in v1:
time: 183 us; the launch traced here: 182 us
  starting transfers between devices  81.7 us (45%)
  waiting for transfers between devices  42.5 us (23%)
  blocking collectives  42.3 us (23%)
  local copies, waits for them, and re-layouts  8.74 us (5%)
  Pallas kernels  3.68 us (2%)
  other arithmetic  2.52 us (1%)
    ppermute x12, starting transfers between devices, route(): return lax.ppermute(value, AXES, pairs)  58.6 us
    ppermute x12, waiting for transfers between devices, route(): return lax.ppermute(value, AXES, pairs)  28.7 us
    all_gather x1, blocking collectives, shards(): parts = lax.all_gather(chip, 'zh')  19.3 us
    all_gather x1, blocking collectives, shards(): grad_parts = lax.all_gather(chip_grad, 'zh')  14 us
    all_to_all x1, starting transfers between devices, shards(): lax.all_to_all(jnp.broadcast_to(row, (256, 1, HIDDEN)), ('zh',) + DOM, 0, 0)  12.3 us
    all_to_all x1, waiting for transfers between devices, shards(): lax.all_to_all(jnp.broadcast_to(row, (256, 1, HIDDEN)), ('zh',) + DOM, 0, 0)  11.2 us
    all_gather x1, blocking collectives, shards(): feature_grad = lax.all_gather(grad_rows, 'c').reshape(ROWS, HIDDEN)  6.48 us
    unnamed x14, local copies, waits for them, and re-layouts  6.47 us
  transfers between devices with their start and end apart: 17, of which 9 were waited for; matrix products, arithmetic and copies ran while one was open for 3% of the time, Pallas kernels for 0%

profile of v1, /device:TPU:1, one launch (start us, length us, event | category | flops | bytes accessed | tf_op | source)
XLA Modules:
  0.0 182.4 jit_solution(2977631768930027670)
XLA Ops:
  0.6 0.0 copy-start
  0.6 8.6 %collective-permute-start = (bf16[512,256]{1,0:T(8,128)(2,1)}, bf16[512,256]{1,0:T(8,128)(2,1)S(1)}, u32[]{:S(2)}, u32[]{:S(2)}) collective-permute-start(bf16[512,256]{1,0:T(8,128)(2,1)} %param.5), channel_id=1, source_target_pairs={{0,8},{1,105},{2,138},{3,235},{4,268},{5,365},{6,398},{7,495},{8,1... | collective-permute-start | bytes 786440 | tf_op jit(solution)/shard_map/ppermute | solution.py:33
  9.2 4.4 %collective-permute-start.2 = (bf16[512,256]{1,0:T(8,128)(2,1)}, bf16[512,256]{1,0:T(8,128)(2,1)S(1)}, u32[]{:S(2)}, u32[]{:S(2)}) collective-permute-start(bf16[512,256]{1,0:T(8,128)(2,1)} %param.5), channel_id=1, source_target_pairs={{0,16},{1,113},{2,146},{3,243},{4,276},{5,373},{6,406},{7,503},{8,... | collective-permute-start | bytes 786440 | tf_op jit(solution)/shard_map/ppermute | solution.py:33
  13.6 3.9 %collective-permute-done.g1 = bf16[512,256]{1,0:T(8,128)(2,1)S(1)} collective-permute-done((bf16[512,256]{1,0:T(8,128)(2,1)}, bf16[512,256]{1,0:T(8,128)(2,1)S(1)}, u32[]{:S(2)}, u32[]{:S(2)}) %collective-permute-start) | collective-permute-done | bytes 262176 | tf_op jit(solution)/shard_map/ppermute | solution.py:33
  17.6 9.6 %collective-permute-start.1 = (bf16[512,256]{1,0:T(8,128)(2,1)S(1)}, bf16[512,256]{1,0:T(8,128)(2,1)S(1)}, u32[]{:S(2)}, u32[]{:S(2)}) collective-permute-start(bf16[512,256]{1,0:T(8,128)(2,1)S(1)} %collective-permute-done.g1), channel_id=1, source_target_pairs={{0,504},{1,505},{2,506},{3,507},{4,508},{5,509},{6,510},{7,511},{8... | collective-permute-start | bytes 786440 | tf_op jit(solution)/shard_map/ppermute | solution.py:33
  27.2 2.9 %collective-permute-done.2.g2 = bf16[512,256]{1,0:T(8,128)(2,1)S(1)} collective-permute-done((bf16[512,256]{1,0:T(8,128)(2,1)}, bf16[512,256]{1,0:T(8,128)(2,1)S(1)}, u32[]{:S(2)}, u32[]{:S(2)}) %collective-permute-start.2) | collective-permute-done | bytes 262176 | tf_op jit(solution)/shard_map/ppermute | solution.py:33
  30.1 1.9 %collective-permute-start.3 = (bf16[512,256]{1,0:T(8,128)(2,1)S(1)}, bf16[512,256]{1,0:T(8,128)(2,1)S(1)}, u32[]{:S(2)}, u32[]{:S(2)}) collective-permute-start(bf16[512,256]{1,0:T(8,128)(2,1)S(1)} %collective-permute-done.2.g2), channel_id=1, source_target_pairs={{0,8},{1,9},{2,10},{3,11},{4,12},{5,13},{6,14},{7,15},{8,16},{9,17... | collective-permute-start | bytes 786440 | tf_op jit(solution)/shard_map/ppermute | solution.py:33
  32.1 1.9 %collective-permute-start.4 = (bf16[1024,256]{1,0:T(8,128)(2,1)S(1)}, bf16[1024,256]{1,0:T(8,128)(2,1)S(1)}, u32[]{:S(2)}, u32[]{:S(2)}) collective-permute-start(bf16[1024,256]{1,0:T(8,128)(2,1)S(1)} %pad_maximum_fusion), channel_id=1, source_target_pairs={{0,65},{1,448},{2,67},{3,450},{4,69},{5,452},{6,71},{7,454},{8,73}... | collective-permute-start | bytes 1572872 | tf_op jit(solution)/shard_map/ppermute | solution.py:33
  34.0 0.0 collective-permute-done.1.g0
  34.0 7.5 %collective-permute-done.3.g3 = bf16[512,256]{1,0:T(8,128)(2,1)S(1)} collective-permute-done((bf16[512,256]{1,0:T(8,128)(2,1)S(1)}, bf16[512,256]{1,0:T(8,128)(2,1)S(1)}, u32[]{:S(2)}, u32[]{:S(2)}) %collective-permute-start.3) | collective-permute-done | bytes 262176 | tf_op jit(solution)/shard_map/ppermute | solution.py:33
  41.6 0.0 copy-start.3
  41.6 0.8 pad_maximum_fusion.1
  42.4 1.9 %collective-permute-start.5 = (bf16[1024,256]{1,0:T(8,128)(2,1)}, bf16[1024,256]{1,0:T(8,128)(2,1)S(1)}, u32[]{:S(2)}, u32[]{:S(2)}) collective-permute-start(bf16[1024,256]{1,0:T(8,128)(2,1)} %pad_maximum_fusion.1), channel_id=1, source_target_pairs={{0,65},{1,448},{2,67},{3,450},{4,69},{5,452},{6,71},{7,454},{8,73}... | collective-permute-start | bytes 1572872 | tf_op jit(solution)/shard_map/ppermute | solution.py:33
  44.3 2.7 %collective-permute-done.4.e12 = bf16[1024,256]{1,0:T(8,128)(2,1)S(1)} collective-permute-done((bf16[1024,256]{1,0:T(8,128)(2,1)S(1)}, bf16[1024,256]{1,0:T(8,128)(2,1)S(1)}, u32[]{:S(2)}, u32[]{:S(2)}) %collective-permute-start.4) | collective-permute-done | bytes 524320 | tf_op jit(solution)/shard_map/ppermute | solution.py:33
  47.1 8.1 %collective-permute-done.5.e03 = bf16[1024,256]{1,0:T(8,128)(2,1)S(1)} collective-permute-done((bf16[1024,256]{1,0:T(8,128)(2,1)}, bf16[1024,256]{1,0:T(8,128)(2,1)S(1)}, u32[]{:S(2)}, u32[]{:S(2)}) %collective-permute-start.5) | collective-permute-done | bytes 524320 | tf_op jit(solution)/shard_map/ppermute | solution.py:33
  55.2 0.0 copy-start.1
  55.2 2.2 %copy-done.1 = bf16[1,8,512,512]{3,2,1,0:T(8,128)(2,1)S(1)} copy-done((bf16[1,8,512,512]{3,2,1,0:T(8,128)(2,1)S(1)}, bf16[1,8,512,512]{3,2,1,0:T(8,128)(2,1)}, u32[]{:S(2)}) %copy-start.1) | copy-done | bytes 4194328
  57.4 0.0 copy-start.4
  57.4 0.7 copy-done.4
  58.1 1.1 shard_map.76
  59.2 1.9 %collective-permute-start.6 = (f32[256,256]{1,0:T(8,128)S(1)}, f32[256,256]{1,0:T(8,128)S(1)}, u32[]{:S(2)}, u32[]{:S(2)}) collective-permute-start(f32[256,256]{1,0:T(8,128)S(1)} %get-tuple-element.10), channel_id=1, source_target_pairs={{0,1},{1,0},{2,3},{3,2},{4,5},{5,4},{6,7},{7,6},{8,9},{9,8},{10,11... | collective-permute-start | bytes 786440 | tf_op jit(solution)/shard_map/ppermute | solution.py:49
  61.1 0.0 copy-done
  61.2 1.5 collective-permute-done.6
  62.7 19.3 %all-gather = bf16[1024,256]{1,0:T(8,128)(2,1)S(1)} all-gather(bf16[256,256]{1,0:T(8,128)(2,1)S(1)} %add_convert_fusion.2), channel_id=2, replica_groups=mesh['zl'=2,'x'=4,'y'=8,'zh'=4,'c'=2] {'zh'}, dimensions={0}, use_global_device_ids=true | all-gather | bytes 655360 | tf_op jit(solution)/shard_map/all_gather | solution.py:180
  82.0 0.0 copy-done.3
  82.0 0.6 shard_map.77
  82.6 2.5 %all-gather.1 = bf16[4,256,256]{2,1,0:T(8,128)(2,1)S(1)} all-gather(bf16[2,256,256]{2,1,0:T(8,128)(2,1)S(1)} %get-tuple-element.11), channel_id=3, replica_groups=mesh['zl'=2,'x'=4,'y'=8,'zh'=4,'c'=2] {'c'}, dimensions={0}, use_global_device_ids=true | all-gather | bytes 786432 | tf_op jit(solution)/shard_map/all_gather | solution.py:193
  85.1 0.0 copy-done.5
  85.1 2.2 %copy-done.2 = bf16[1,8,512,512]{3,2,1,0:T(8,128)(2,1)S(1)} copy-done((bf16[1,8,512,512]{3,2,1,0:T(8,128)(2,1)S(1)}, bf16[1,8,512,512]{3,2,1,0:T(8,128)(2,1)}, u32[]{:S(2)}) %copy-start.2) | copy-done | bytes 4194328
  87.3 1.0 shard_map.79
  88.3 1.9 %collective-permute-start.8 = (bf16[2,2,256,256]{3,2,1,0:T(8,128)(2,1)S(1)}, bf16[2,2,256,256]{3,2,1,0:T(8,128)(2,1)S(1)}, u32[]{:S(2)}, u32[]{:S(2)}) collective-permute-start(bf16[2,2,256,256]{3,2,1,0:T(8,128)(2,1)S(1)} %shard_map.79), channel_id=1, source_target_pairs={{0,65},{1,448},{2,67},{3,450},{4,69},{5,452},{6,71},{7,454},{8,73}... | collective-permute-start | bytes 1572872 | tf_op jit(solution)/shard_map/ppermute | solution.py:33
  90.2 0.8 shard_map.78
  91.0 6.4 %collective-permute-start.7 = (bf16[2,2,256,256]{3,2,1,0:T(8,128)(2,1)S(1)}, bf16[2,2,256,256]{3,2,1,0:T(8,128)(2,1)S(1)}, u32[]{:S(2)}, u32[]{:S(2)}) collective-permute-start(bf16[2,2,256,256]{3,2,1,0:T(8,128)(2,1)S(1)} %get-tuple-element.13), channel_id=1, source_target_pairs={{0,65},{1,448},{2,67},{3,450},{4,69},{5,452},{6,71},{7,454},{8,73}... | collective-permute-start | bytes 1572872 | tf_op jit(solution)/shard_map/ppermute | solution.py:33
  97.4 3.4 %collective-permute-done.8 = bf16[2,2,256,256]{3,2,1,0:T(8,128)(2,1)S(1)} collective-permute-done((bf16[2,2,256,256]{3,2,1,0:T(8,128)(2,1)S(1)}, bf16[2,2,256,256]{3,2,1,0:T(8,128)(2,1)S(1)}, u32[]{:S(2)}, u32[]{:S(2)}) %collective-permute-start.8) | collective-permute-done | bytes 524320 | tf_op jit(solution)/shard_map/ppermute | solution.py:33
  100.9 0.1 fusion.2
  101.0 1.9 %collective-permute-start.9 = (bf16[2,256,256]{2,1,0:T(8,128)(2,1)S(1)}, bf16[2,256,256]{2,1,0:T(8,128)(2,1)}, u32[]{:S(2)}, u32[]{:S(2)}) collective-permute-start(bf16[2,256,256]{2,1,0:T(8,128)(2,1)S(1)} %get-tuple-element.17), channel_id=1, source_target_pairs={{0,8},{1,9},{2,10},{3,11},{4,12},{5,13},{6,14},{7,15},{8,16},{9,17... | collective-permute-start | bytes 786440 | tf_op jit(solution)/shard_map/ppermute | solution.py:33
  103.0 7.6 %collective-permute-start.11 = (bf16[2,256,256]{2,1,0:T(8,128)(2,1)S(1)}, bf16[2,256,256]{2,1,0:T(8,128)(2,1)}, u32[]{:S(2)}, u32[]{:S(2)}) collective-permute-start(bf16[2,256,256]{2,1,0:T(8,128)(2,1)S(1)} %get-tuple-element.18), channel_id=1, source_target_pairs={{0,504},{1,505},{2,506},{3,507},{4,508},{5,509},{6,510},{7,511},{8... | collective-permute-start | bytes 786440 | tf_op jit(solution)/shard_map/ppermute | solution.py:33
  110.5 0.7 copy.8
  111.2 4.6 %all-to-all-start = ((f32[64,1,256]{2,1,0:T(1,128)}), f32[64,1,256]{2,1,0:T(1,128)S(1)}, u32[]{:S(2)}, u32[]{:S(2)}) async-start(f32[64,1,256]{2,1,0:T(1,128)} %copy.8), calls=%async_computation | async-start | bytes 131072 | tf_op jit(solution)/shard_map/all_to_all | solution.py:222
  115.9 0.0 collective-permute-done.7
  115.9 0.0 collective-permute-done.9
  115.9 0.0 collective-permute-done.11
  115.9 1.2 fusion.1
  117.1 7.3 %collective-permute-start.12 = (bf16[2,256,256]{2,1,0:T(8,128)(2,1)S(1)}, bf16[2,256,256]{2,1,0:T(8,128)(2,1)S(1)}, u32[]{:S(2)}, u32[]{:S(2)}) collective-permute-start(bf16[2,256,256]{2,1,0:T(8,128)(2,1)S(1)} %get-tuple-element.16), channel_id=1, source_target_pairs={{0,496},{1,401},{2,370},{3,275},{4,244},{5,149},{6,118},{7,23},{8,... | collective-permute-start | bytes 786440 | tf_op jit(solution)/shard_map/ppermute | solution.py:33
  124.5 5.1 %collective-permute-start.10 = (bf16[2,256,256]{2,1,0:T(8,128)(2,1)S(1)}, bf16[2,256,256]{2,1,0:T(8,128)(2,1)S(1)}, u32[]{:S(2)}, u32[]{:S(2)}) collective-permute-start(bf16[2,256,256]{2,1,0:T(8,128)(2,1)S(1)} %get-tuple-element.15), channel_id=1, source_target_pairs={{0,504},{1,409},{2,378},{3,283},{4,252},{5,157},{6,126},{7,31},{8,... | collective-permute-start | bytes 786440 | tf_op jit(solution)/shard_map/ppermute | solution.py:33
  129.6 0.0 all-to-all-done
  129.6 0.1 reduce_sum.11
  129.7 1.9 %collective-permute-start.14 = (f32[1,256]{1,0:T(1,128)S(1)}, f32[1,256]{1,0:T(1,128)S(1)}, u32[]{:S(2)}, u32[]{:S(2)}) collective-permute-start(f32[1,256]{1,0:T(1,128)S(1)} %bitcast.38), channel_id=1, source_target_pairs={{0,1},{1,0},{2,3},{3,2},{4,5},{5,4},{6,7},{7,6},{8,9},{9,8},{10,11... | collective-permute-start | bytes 3080 | tf_op jit(solution)/shard_map/ppermute | solution.py:49
  131.6 1.1 collective-permute-done.14
  132.7 0.8 broadcast_in_dim.3
  133.6 12.3 %all-to-all-start.1 = ((f32[256,1,256]{2,1,0:T(1,128)}), f32[256,1,256]{2,1,0:T(1,128)S(1)}, u32[]{:S(2)}, u32[]{:S(2)}) async-start(f32[256,1,256]{2,1,0:T(1,128)} %broadcast_in_dim.3), calls=%async_computation.1 | async-start | bytes 524288 | tf_op jit(solution)/shard_map/all_to_all | solution.py:225
  145.9 0.0 collective-permute-done.12
  145.9 0.0 collective-permute-done.10
  145.9 0.1 convert_add_fusion
  146.0 2.4 %collective-permute-start.13 = (f32[256,256]{1,0:T(8,128)S(1)}, f32[256,256]{1,0:T(8,128)S(1)}, u32[]{:S(2)}, u32[]{:S(2)}) collective-permute-start(f32[256,256]{1,0:T(8,128)S(1)} %select_bitcast_fusion), channel_id=1, source_target_pairs={{0,1},{1,0},{2,3},{3,2},{4,5},{5,4},{6,7},{7,6},{8,9},{9,8},{10,11... | collective-permute-start | bytes 786440 | tf_op jit(solution)/shard_map/ppermute | solution.py:49
  148.4 0.7 slice.46
  149.1 11.2 %all-to-all-done.1 = f32[256,1,256]{2,1,0:T(1,128)S(1)} async-done(((f32[256,1,256]{2,1,0:T(1,128)}), f32[256,1,256]{2,1,0:T(1,128)S(1)}, u32[]{:S(2)}, u32[]{:S(2)}) %all-to-all-start.1) | async-done | bytes 262176 | tf_op jit(solution)/shard_map/all_to_all | solution.py:225
  160.3 0.7 copy.11
  161.1 0.0 collective-permute-done.13
  161.1 0.1 fusion.4
  161.1 14.0 %all-gather.2 = bf16[1024,256]{1,0:T(8,128)(2,1)S(1)} all-gather(bf16[256,256]{1,0:T(8,128)(2,1)S(1)} %fusion.4), channel_id=4, replica_groups=mesh['zl'=2,'x'=4,'y'=8,'zh'=4,'c'=2] {'zh'}, dimensions={0}, use_global_device_ids=true | all-gather | bytes 655360 | tf_op jit(solution)/shard_map/all_gather | solution.py:212
  175.1 0.1 shard_map.80
  175.2 6.5 %all-gather.3 = bf16[512,256]{1,0:T(8,128)(2,1)S(1)} all-gather(bf16[256,256]{1,0:T(8,128)(2,1)S(1)} %shard_map.80), channel_id=5, replica_groups=mesh['zl'=2,'x'=4,'y'=8,'zh'=4,'c'=2] {'c'}, dimensions={0}, use_global_device_ids=true | all-gather | bytes 393216 | tf_op jit(solution)/shard_map/all_gather | solution.py:220
  181.7 0.7 copy.13
  (7 shorter events, 0.1 us)
Async XLA Ops:
  0.6 60.5 %copy-start = (bf16[512,256]{1,0:T(8,128)(2,1)S(1)}, bf16[512,256]{1,0:T(8,128)(2,1)}, u32[]{:S(2)}) copy-start(bf16[512,256]{1,0:T(8,128)(2,1)} %param.7) | copy-start | bytes 786436
  0.6 16.9 %collective-permute-start = (bf16[512,256]{1,0:T(8,128)(2,1)}, bf16[512,256]{1,0:T(8,128)(2,1)S(1)}, u32[]{:S(2)}, u32[]{:S(2)}) collective-permute-start(bf16[512,256]{1,0:T(8,128)(2,1)} %param.5), channel_id=1, source_target_pairs={{0,8},{1,105},{2,138},{3,235},{4,268},{5,365},{6,398},{7,495},{8,1... | collective-permute-start | bytes 786440 | tf_op jit(solution)/shard_map/ppermute | solution.py:33
  9.2 20.9 %collective-permute-start.2 = (bf16[512,256]{1,0:T(8,128)(2,1)}, bf16[512,256]{1,0:T(8,128)(2,1)S(1)}, u32[]{:S(2)}, u32[]{:S(2)}) collective-permute-start(bf16[512,256]{1,0:T(8,128)(2,1)} %param.5), channel_id=1, source_target_pairs={{0,16},{1,113},{2,146},{3,243},{4,276},{5,373},{6,406},{7,503},{8,... | collective-permute-start | bytes 786440 | tf_op jit(solution)/shard_map/ppermute | solution.py:33
  17.6 16.5 %collective-permute-start.1 = (bf16[512,256]{1,0:T(8,128)(2,1)S(1)}, bf16[512,256]{1,0:T(8,128)(2,1)S(1)}, u32[]{:S(2)}, u32[]{:S(2)}) collective-permute-start(bf16[512,256]{1,0:T(8,128)(2,1)S(1)} %collective-permute-done.g1), channel_id=1, source_target_pairs={{0,504},{1,505},{2,506},{3,507},{4,508},{5,509},{6,510},{7,511},{8... | collective-permute-start | bytes 786440 | tf_op jit(solution)/shard_map/ppermute | solution.py:33
  30.1 11.4 %collective-permute-start.3 = (bf16[512,256]{1,0:T(8,128)(2,1)S(1)}, bf16[512,256]{1,0:T(8,128)(2,1)S(1)}, u32[]{:S(2)}, u32[]{:S(2)}) collective-permute-start(bf16[512,256]{1,0:T(8,128)(2,1)S(1)} %collective-permute-done.2.g2), channel_id=1, source_target_pairs={{0,8},{1,9},{2,10},{3,11},{4,12},{5,13},{6,14},{7,15},{8,16},{9,17... | collective-permute-start | bytes 786440 | tf_op jit(solution)/shard_map/ppermute | solution.py:33
  32.1 15.0 %collective-permute-start.4 = (bf16[1024,256]{1,0:T(8,128)(2,1)S(1)}, bf16[1024,256]{1,0:T(8,128)(2,1)S(1)}, u32[]{:S(2)}, u32[]{:S(2)}) collective-permute-start(bf16[1024,256]{1,0:T(8,128)(2,1)S(1)} %pad_maximum_fusion), channel_id=1, source_target_pairs={{0,65},{1,448},{2,67},{3,450},{4,69},{5,452},{6,71},{7,454},{8,73}... | collective-permute-start | bytes 1572872 | tf_op jit(solution)/shard_map/ppermute | solution.py:33
  41.6 40.4 %copy-start.3 = (bf16[256,256]{1,0:T(8,128)(2,1)S(1)}, bf16[256,256]{1,0:T(8,128)(2,1)}, u32[]{:S(2)}) copy-start(bf16[256,256]{1,0:T(8,128)(2,1)} %weight_ref.1) | copy-start | bytes 393220
  42.4 12.8 %collective-permute-start.5 = (bf16[1024,256]{1,0:T(8,128)(2,1)}, bf16[1024,256]{1,0:T(8,128)(2,1)S(1)}, u32[]{:S(2)}, u32[]{:S(2)}) collective-permute-start(bf16[1024,256]{1,0:T(8,128)(2,1)} %pad_maximum_fusion.1), channel_id=1, source_target_pairs={{0,65},{1,448},{2,67},{3,450},{4,69},{5,452},{6,71},{7,454},{8,73}... | collective-permute-start | bytes 1572872 | tf_op jit(solution)/shard_map/ppermute | solution.py:33
  55.2 2.2 %copy-start.1 = (bf16[1,8,512,512]{3,2,1,0:T(8,128)(2,1)S(1)}, bf16[1,8,512,512]{3,2,1,0:T(8,128)(2,1)}, u32[]{:S(2)}) copy-start(bf16[1,8,512,512]{3,2,1,0:T(8,128)(2,1)} %tiles_ref.5) | copy-start | bytes 12582916
  57.4 0.7 copy-start.4
  58.1 27.0 %copy-start.5 = (s32[1,8]{1,0:T(1,128)S(1)}, s32[1,8]{1,0:T(1,128)}, u32[]{:S(2)}) copy-start(s32[1,8]{1,0:T(1,128)} %mask_ref.5) | copy-start | bytes 100
  59.2 3.4 %collective-permute-start.6 = (f32[256,256]{1,0:T(8,128)S(1)}, f32[256,256]{1,0:T(8,128)S(1)}, u32[]{:S(2)}, u32[]{:S(2)}) collective-permute-start(f32[256,256]{1,0:T(8,128)S(1)} %get-tuple-element.10), channel_id=1, source_target_pairs={{0,1},{1,0},{2,3},{3,2},{4,5},{5,4},{6,7},{7,6},{8,9},{9,8},{10,11... | collective-permute-start | bytes 786440 | tf_op jit(solution)/shard_map/ppermute | solution.py:49
  85.1 2.2 %copy-start.2 = (bf16[1,8,512,512]{3,2,1,0:T(8,128)(2,1)S(1)}, bf16[1,8,512,512]{3,2,1,0:T(8,128)(2,1)}, u32[]{:S(2)}) copy-start(bf16[1,8,512,512]{3,2,1,0:T(8,128)(2,1)} %tiles_ref.5) | copy-start | bytes 12582916
  88.3 12.6 %collective-permute-start.8 = (bf16[2,2,256,256]{3,2,1,0:T(8,128)(2,1)S(1)}, bf16[2,2,256,256]{3,2,1,0:T(8,128)(2,1)S(1)}, u32[]{:S(2)}, u32[]{:S(2)}) collective-permute-start(bf16[2,2,256,256]{3,2,1,0:T(8,128)(2,1)S(1)} %shard_map.79), channel_id=1, source_target_pairs={{0,65},{1,448},{2,67},{3,450},{4,69},{5,452},{6,71},{7,454},{8,73}... | collective-permute-start | bytes 1572872 | tf_op jit(solution)/shard_map/ppermute | solution.py:33
  91.0 24.8 %collective-permute-start.7 = (bf16[2,2,256,256]{3,2,1,0:T(8,128)(2,1)S(1)}, bf16[2,2,256,256]{3,2,1,0:T(8,128)(2,1)S(1)}, u32[]{:S(2)}, u32[]{:S(2)}) collective-permute-start(bf16[2,2,256,256]{3,2,1,0:T(8,128)(2,1)S(1)} %get-tuple-element.13), channel_id=1, source_target_pairs={{0,65},{1,448},{2,67},{3,450},{4,69},{5,452},{6,71},{7,454},{8,73}... | collective-permute-start | bytes 1572872 | tf_op jit(solution)/shard_map/ppermute | solution.py:33
  101.0 14.9 %collective-permute-start.9 = (bf16[2,256,256]{2,1,0:T(8,128)(2,1)S(1)}, bf16[2,256,256]{2,1,0:T(8,128)(2,1)}, u32[]{:S(2)}, u32[]{:S(2)}) collective-permute-start(bf16[2,256,256]{2,1,0:T(8,128)(2,1)S(1)} %get-tuple-element.17), channel_id=1, source_target_pairs={{0,8},{1,9},{2,10},{3,11},{4,12},{5,13},{6,14},{7,15},{8,16},{9,17... | collective-permute-start | bytes 786440 | tf_op jit(solution)/shard_map/ppermute | solution.py:33
  103.0 12.9 %collective-permute-start.11 = (bf16[2,256,256]{2,1,0:T(8,128)(2,1)S(1)}, bf16[2,256,256]{2,1,0:T(8,128)(2,1)}, u32[]{:S(2)}, u32[]{:S(2)}) collective-permute-start(bf16[2,256,256]{2,1,0:T(8,128)(2,1)S(1)} %get-tuple-element.18), channel_id=1, source_target_pairs={{0,504},{1,505},{2,506},{3,507},{4,508},{5,509},{6,510},{7,511},{8... | collective-permute-start | bytes 786440 | tf_op jit(solution)/shard_map/ppermute | solution.py:33
  111.2 18.4 %all-to-all-start = ((f32[64,1,256]{2,1,0:T(1,128)}), f32[64,1,256]{2,1,0:T(1,128)S(1)}, u32[]{:S(2)}, u32[]{:S(2)}) async-start(f32[64,1,256]{2,1,0:T(1,128)} %copy.8), calls=%async_computation | async-start | bytes 131072 | tf_op jit(solution)/shard_map/all_to_all | solution.py:222
  117.1 28.7 %collective-permute-start.12 = (bf16[2,256,256]{2,1,0:T(8,128)(2,1)S(1)}, bf16[2,256,256]{2,1,0:T(8,128)(2,1)S(1)}, u32[]{:S(2)}, u32[]{:S(2)}) collective-permute-start(bf16[2,256,256]{2,1,0:T(8,128)(2,1)S(1)} %get-tuple-element.16), channel_id=1, source_target_pairs={{0,496},{1,401},{2,370},{3,275},{4,244},{5,149},{6,118},{7,23},{8,... | collective-permute-start | bytes 786440 | tf_op jit(solution)/shard_map/ppermute | solution.py:33
  124.5 21.4 %collective-permute-start.10 = (bf16[2,256,256]{2,1,0:T(8,128)(2,1)S(1)}, bf16[2,256,256]{2,1,0:T(8,128)(2,1)S(1)}, u32[]{:S(2)}, u32[]{:S(2)}) collective-permute-start(bf16[2,256,256]{2,1,0:T(8,128)(2,1)S(1)} %get-tuple-element.15), channel_id=1, source_target_pairs={{0,504},{1,409},{2,378},{3,283},{4,252},{5,157},{6,126},{7,31},{8,... | collective-permute-start | bytes 786440 | tf_op jit(solution)/shard_map/ppermute | solution.py:33
  129.7 3.0 %collective-permute-start.14 = (f32[1,256]{1,0:T(1,128)S(1)}, f32[1,256]{1,0:T(1,128)S(1)}, u32[]{:S(2)}, u32[]{:S(2)}) collective-permute-start(f32[1,256]{1,0:T(1,128)S(1)} %bitcast.38), channel_id=1, source_target_pairs={{0,1},{1,0},{2,3},{3,2},{4,5},{5,4},{6,7},{7,6},{8,9},{9,8},{10,11... | collective-permute-start | bytes 3080 | tf_op jit(solution)/shard_map/ppermute | solution.py:49
  133.6 26.8 %all-to-all-start.1 = ((f32[256,1,256]{2,1,0:T(1,128)}), f32[256,1,256]{2,1,0:T(1,128)S(1)}, u32[]{:S(2)}, u32[]{:S(2)}) async-start(f32[256,1,256]{2,1,0:T(1,128)} %broadcast_in_dim.3), calls=%async_computation.1 | async-start | bytes 524288 | tf_op jit(solution)/shard_map/all_to_all | solution.py:225
  146.0 15.1 %collective-permute-start.13 = (f32[256,256]{1,0:T(8,128)S(1)}, f32[256,256]{1,0:T(8,128)S(1)}, u32[]{:S(2)}, u32[]{:S(2)}) collective-permute-start(f32[256,256]{1,0:T(8,128)S(1)} %select_bitcast_fusion), channel_id=1, source_target_pairs={{0,1},{1,0},{2,3},{3,2},{4,5},{5,4},{6,7},{7,6},{8,9},{9,8},{10,11... | collective-permute-start | bytes 786440 | tf_op jit(solution)/shard_map/ppermute | solution.py:49

commit v2 on v1

v2 whole, which is shorter than its diff:
```python
import functools

import jax
import jax.numpy as jnp
from jax import lax
from jax.experimental import pallas as pl
from jax.experimental.pallas import tpu as pltpu
from jax.sharding import Mesh
from jax.sharding import PartitionSpec as P

AXES = ("zl", "x", "y", "zh", "c")
SIZES = (2, 4, 8, 4, 2)
DOM = ("zl", "x", "y")
BLOCKS = 64
REPLICAS = 8
ROWS = 512
HALF = 256
HIDDEN = 256
F32 = jnp.float32
BF16 = jnp.bfloat16
SMEM = pl.BlockSpec(memory_space=pltpu.SMEM)
VMEM = pl.BlockSpec(memory_space=pltpu.VMEM)
HBM = pl.BlockSpec(memory_space=pltpu.HBM)
PARAMS = pltpu.CompilerParams(vmem_limit_bytes=24 * 1024 * 1024)
WIDE_PARAMS = pltpu.CompilerParams(vmem_limit_bytes=60 * 1024 * 1024)


def route(value, target):
    pairs = []
    for i in range(BLOCKS):
        for r in range(REPLICAS):
            i2, r2 = target(i, r)
            pairs.append((i * REPLICAS + r, (i2 % BLOCKS) * REPLICAS + r2 % REPLICAS))
    return lax.ppermute(value, AXES, pairs)


def partner(i, r):
    return (i + 8, r + 1) if r % 2 == 0 else (i - 8, r - 1)


def swap_pair(value):
    return route(value, partner)


def side(r):
    return 1 - 2 * (r % 2)


def offsets_of(core, pair, slot):
    return (7 * core, 1 + 5 * core, 2 + 3 * core, 3 + core)[2 * pair + slot]


def load_kernel(mask_ref, tiles_ref, held_ref, sems):
    def copy(t):
        return pltpu.make_async_copy(tiles_ref.at[0, t], held_ref.at[t], sems.at[t])

    for t in range(8):

        @pl.when(mask_ref[0, t] > 0)
        def _():
            copy(t).start()

    for t in range(8):

        @pl.when(mask_ref[0, t] > 0)
        def _():
            copy(t).wait()


def tile_steps(core_ref, mask_ref, held, work, present, absent):
    core = core_ref[0]
    for step, (member, pair, slot) in enumerate(work):
        t = offsets_of(core if member == 0 else 1 - core, pair, slot)

        @pl.when(mask_ref[0, t] > 0)
        def _():
            present(step, held.at[t])

        if absent is not None:

            @pl.when(mask_ref[0, t] == 0)
            def _():
                absent(step)


def early_kernel(core_ref, mask_ref, held, own0, other0, own1, acc):
    blocks = (own0, other0, own1)
    acc[...] = jnp.zeros_like(acc)

    def present(step, tile):
        start = (step % 2) * ROWS
        acc[...] += jnp.dot(tile[...], blocks[step // 2][start : start + ROWS, :], preferred_element_type=F32)

    work = [(member, pair, slot) for member, pair in ((0, 0), (1, 0), (0, 1)) for slot in range(2)]
    tile_steps(core_ref, mask_ref, held, work, present, None)


def late_kernel(core_ref, mask_ref, held, before, other1, keep_ref, send_ref, acc):
    core = core_ref[0]
    acc[...] = before[...]

    def present(step, tile):
        acc[...] += jnp.dot(tile[...], other1[step * ROWS : (step + 1) * ROWS, :], preferred_element_type=F32)

    tile_steps(core_ref, mask_ref, held, [(1, 1, 0), (1, 1, 1)], present, None)
    keep_ref[...] = acc[pl.ds(pl.multiple_of(core * HALF, HALF), HALF), :]
    send_ref[...] = acc[pl.ds(pl.multiple_of(HALF - core * HALF, HALF), HALF), :]


def middle_kernel(zh_ref, parts_ref, weight_ref, grad_ref, pack_ref, full):
    wide = parts_ref[0].astype(F32)
    for s in range(1, 4):
        wide = wide + parts_ref[s].astype(F32)
    high = wide.astype(BF16)
    low = (wide - high.astype(F32)).astype(BF16)
    weight = weight_ref[...]
    total = jnp.dot(high, weight, preferred_element_type=F32) + jnp.dot(low, weight, preferred_element_type=F32)
    gate = jax.nn.sigmoid(total)
    pack_ref[:HALF] = (total * gate).astype(BF16)
    score = (grad_ref[...].astype(F32) * gate * (1.0 + total * (1.0 - gate))).astype(BF16)
    turned = lax.dot_general(weight, score, (((1,), (1,)), ((), ())), preferred_element_type=F32)
    pack_ref[HALF : 2 * HALF] = turned.astype(BF16)
    full[...] = lax.dot_general(high, score, (((0,), (0,)), ((), ())), preferred_element_type=F32)
    term = full[pl.ds(pl.multiple_of(zh_ref[0] * 64, 64), 64), :]
    term_high = term.astype(BF16)
    pack_ref[512:576] = term_high
    pack_ref[576:640] = (term - term_high.astype(F32)).astype(BF16)


def backward_kernel(plan, core_ref, mask_ref, held, pack_ref, *outs):
    def present(step, tile):
        value = jnp.dot(pack_ref[0, HALF : 2 * HALF], tile[:HALF, :], preferred_element_type=F32)
        value = value + jnp.dot(pack_ref[1, HALF : 2 * HALF], tile[HALF:, :], preferred_element_type=F32)
        value = value.astype(BF16)
        outs[step // 2][step % 2, 0] = value[:, :HALF]
        outs[step // 2][step % 2, 1] = value[:, HALF:]

    def absent(step):
        outs[step // 2][step % 2] = jnp.zeros((2, HIDDEN, HALF), BF16)

    work = [(member, pair, slot) for member, pair in plan for slot in range(2)]
    tile_steps(core_ref, mask_ref, held, work, present, absent)


def turn_kernel(parts_ref, out_ref):
    wide = parts_ref[0, :HALF].astype(F32)
    for s in range(1, 4):
        wide = wide + parts_ref[s, :HALF].astype(F32)
    out_ref[:HALF] = wide.T.astype(BF16)
    for s in range(4):
        out_ref[HALF + 32 * s : HALF + 32 * (s + 1)] = parts_ref[s, HALF:]


def last_kernel(packs_ref, rows_ref, weight_ref):
    for c in range(2):
        rows_ref[c * HALF : (c + 1) * HALF] = packs_ref[c, :HALF]
        for s in range(4):
            start = HALF + 32 * s
            weight_ref[64 * s + 32 * c : 64 * s + 32 * c + 32] = packs_ref[c, start : start + 32].astype(F32)


def products(plan, core, mask, held, packs):
    return pl.pallas_call(
        functools.partial(backward_kernel, plan),
        out_shape=[jax.ShapeDtypeStruct((2, 2, HIDDEN, HALF), BF16) for _ in plan],
        in_specs=[SMEM, SMEM, VMEM, VMEM],
        out_specs=[VMEM] * len(plan),
        compiler_params=PARAMS,
        cost_estimate=pl.CostEstimate(flops=2 * 10**9, bytes_accessed=6 * 2**20, transcendentals=0),
    )(core, mask, held, packs)


def total_of(*values):
    wide = values[0].astype(F32)
    for value in values[1:]:
        wide = wide + value.astype(F32)
    return wide


def spread_sum(value, axes):
    copies = jnp.broadcast_to(value, (8,) + value.shape)
    return jnp.sum(lax.all_to_all(copies, axes, 0, 0), axis=0)


def shards(features, weight, grad_out, tiles, tile_mask):
    core_index = lax.axis_index("c")
    core = core_index.astype(jnp.int32).reshape(1)
    zh = lax.axis_index("zh").astype(jnp.int32).reshape(1)
    even = core_index == 0

    held = pl.pallas_call(
        load_kernel,
        out_shape=jax.ShapeDtypeStruct((8, ROWS, ROWS), BF16),
        in_specs=[SMEM, HBM],
        out_specs=VMEM,
        scratch_shapes=[pltpu.SemaphoreType.DMA((8,))],
        compiler_params=WIDE_PARAMS,
    )(tile_mask, tiles)
    fetched1 = route(features, lambda i, r: (i + 8 * r + 2 + 3 * (r % 2), r))
    fetched0 = route(features, lambda i, r: (i + 8 * r + 7 * (r % 2), r))
    own0 = jnp.concatenate([fetched0, route(fetched0, lambda i, r: (i + side(r), r))])
    own1 = jnp.concatenate([fetched1, route(fetched1, lambda i, r: (i + side(r), r))])
    other0 = swap_pair(own0)
    other1 = swap_pair(own1)
    half = jax.ShapeDtypeStruct((HALF, HIDDEN), F32)
    before = pl.pallas_call(
        early_kernel,
        out_shape=jax.ShapeDtypeStruct((ROWS, HIDDEN), F32),
        in_specs=[SMEM, SMEM] + [VMEM] * 4,
        out_specs=VMEM,
        compiler_params=PARAMS,
        cost_estimate=pl.CostEstimate(flops=2 * 10**9, bytes_accessed=6 * 2**20, transcendentals=0),
    )(core, tile_mask, held, own0, other0, own1)
    keep, send = pl.pallas_call(
        late_kernel,
        out_shape=[half, half],
        in_specs=[SMEM, SMEM] + [VMEM] * 3,
        out_specs=[VMEM, VMEM],
        scratch_shapes=[pltpu.VMEM((ROWS, HIDDEN), F32)],
        compiler_params=PARAMS,
    )(core, tile_mask, held, before, other1)
    sent = lax.all_gather(send, "c")
    chip = (keep + jnp.where(even, sent[1], sent[0])).astype(BF16)
    parts = lax.all_gather(chip, "zh")
    grad_half = lax.dynamic_slice_in_dim(grad_out, core_index * HALF, HALF, 0)
    pack = pl.pallas_call(
        middle_kernel,
        out_shape=jax.ShapeDtypeStruct((640, HIDDEN), BF16),
        in_specs=[SMEM] + [VMEM] * 3,
        out_specs=VMEM,
        scratch_shapes=[pltpu.VMEM((HIDDEN, HIDDEN), F32)],
        compiler_params=PARAMS,
    )(zh, parts, weight, grad_half)
    packs = lax.all_gather(pack, "c")
    activated = packs[:, :HALF].reshape(ROWS, HIDDEN)

    (send1,) = products(((1, 1),), core, tile_mask, held, packs)
    got1 = swap_pair(send1)
    send0, mine0, mine1 = products(((1, 0), (0, 0), (0, 1)), core, tile_mask, held, packs)
    got0 = swap_pair(send0)
    back1 = route(total_of(mine1[1], got1[1]).astype(BF16), lambda i, r: (i - side(r), r))
    back0 = route(total_of(mine0[1], got0[1]).astype(BF16), lambda i, r: (i - side(r), r))
    far = total_of(mine1[0], got1[0], back1).astype(BF16)
    home_far = route(far, lambda i, r: (i - 8 * r - 2 - 3 * (r % 2), r))
    near = total_of(mine0[0], got0[0], back0).astype(BF16)
    home_near = route(near, lambda i, r: (i - 8 * r - 7 * (r % 2), r))

    high, low = packs[:, 512:576].astype(F32), packs[:, 576:640].astype(F32)
    term = lax.dynamic_slice_in_dim(high[0] + low[0] + (high[1] + low[1]), core_index * 32, 32, 0)
    term = spread_sum(term, "y")
    term, _ = lax.optimization_barrier((term, far))
    term = (spread_sum(term, ("zl", "x")) * (BLOCKS * ROWS) ** -0.5).astype(BF16)

    flipped = total_of(jnp.where(even, home_near[1], home_near[0]), jnp.where(even, home_far[1], home_far[0]))
    kept = total_of(jnp.where(even, home_near[0], home_near[1]), jnp.where(even, home_far[0], home_far[1]))
    crossed = lax.all_gather(flipped, "c")
    chip_grad = (kept + jnp.where(even, crossed[1], crossed[0])).astype(BF16)
    grad_parts = lax.all_gather(jnp.concatenate([chip_grad, term]), "zh")
    turned = pl.pallas_call(
        turn_kernel,
        out_shape=jax.ShapeDtypeStruct((HALF + 128, HIDDEN), BF16),
        in_specs=[VMEM],
        out_specs=VMEM,
        compiler_params=PARAMS,
    )(grad_parts)
    feature_grad, weight_grad = pl.pallas_call(
        last_kernel,
        out_shape=[jax.ShapeDtypeStruct((ROWS, HIDDEN), BF16), jax.ShapeDtypeStruct((HIDDEN, HIDDEN), F32)],
        in_specs=[VMEM],
        out_specs=[VMEM, VMEM],
        compiler_params=PARAMS,
    )(lax.all_gather(turned, "c"))
    return activated, feature_grad, weight_grad


def solution(mesh):
    fine = Mesh(mesh.devices.reshape(SIZES), AXES)
    nodes = P(DOM, None)
    return jax.shard_map(
        shards,
        mesh=fine,
        in_specs=(nodes, P(), nodes, P(DOM, ("zh", "c"), None, None), P(DOM, ("zh", "c"))),
        out_specs=(nodes, nodes, P()),
        check_vma=False,
    )
```

time: 183 us -> 152 us (0.83)
  starting transfers between devices: 81.7 us -> 61.7 us
  waiting for transfers between devices: 42.5 us -> 23.6 us
  blocking collectives: 42.3 us -> 47.5 us
  Pallas kernels: 3.68 us -> 8.52 us
  local copies, waits for them, and re-layouts: 8.74 us -> 4.5 us
    all_to_all x2, waiting for transfers between devices: 11.2 us -> 0.91 us  [spread_sum(): return jnp.sum(lax.all_to_all(copies, axes, 0, 0), axis=0)]
    all_to_all x2, starting transfers between devices: 16.9 us -> 7.96 us  [spread_sum(): return jnp.sum(lax.all_to_all(copies, axes, 0, 0), axis=0)]
    ppermute x3 -> x0, starting transfers between devices: 6.22 us -> none  [swap_core(): return lax.ppermute(value, 'c', [(0, 1), (1, 0)])]
    ppermute x12, waiting for transfers between devices: 28.7 us -> 22.7 us  [route(): return lax.ppermute(value, AXES, pairs)]
    pallas_call x3 -> x6, Pallas kernels: 1.84 us -> 6.91 us  [the longest x1 3.86 us: shards(): pl.pallas_call(load_kernel, out_shape=jax.ShapeDtypeStruct((8, ROWS, ROWS...]
    ppermute x12, starting transfers between devices: 58.6 us -> 53.7 us  [route(): return lax.ppermute(value, AXES, pairs)]
    unnamed x14 -> x12, local copies, waits for them, and re-layouts: 6.47 us -> 2.25 us
    all_gather x2 -> x4, blocking collectives: 20.5 us -> 24.1 us  [the longest x1 16.1 us: shards(): grad_parts = lax.all_gather(jnp.concatenate([chip_grad, term]), 'zh')]
  transfers between devices with their start and end apart: 17 -> 14, of which waited for: 9 -> 9; matrix products, arithmetic and copies ran while one was open for 3% -> 4% of each run, Pallas kernels for 0% -> 4%
where the time goes in v2:
time: 152 us; the launch traced here: 151 us
  starting transfers between devices  61.7 us (41%)
  blocking collectives  47.5 us (31%)
  waiting for transfers between devices  23.6 us (16%)
  Pallas kernels  8.52 us (6%)
  local copies, waits for them, and re-layouts  4.5 us (3%)
  other arithmetic  3.96 us (3%)
    ppermute x12, starting transfers between devices, route(): return lax.ppermute(value, AXES, pairs)  53.7 us
    ppermute x12, waiting for transfers between devices, route(): return lax.ppermute(value, AXES, pairs)  22.7 us
    all_gather x1, blocking collectives, shards(): parts = lax.all_gather(chip, 'zh')  20.4 us
    all_gather x1, blocking collectives, shards(): grad_parts = lax.all_gather(jnp.concatenate([chip_grad, term]), 'zh')  16.1 us
    all_to_all x2, starting transfers between devices, spread_sum(): return jnp.sum(lax.all_to_all(copies, axes, 0, 0), axis=0)  7.96 us
    pallas_call x1, Pallas kernels, shards(): pl.pallas_call(load_kernel, out_shape=jax.ShapeDtypeStruct((8, ROWS, ROWS...  3.86 us
    all_gather x1, blocking collectives, shards(): lax.all_gather(turned, 'c')  3.59 us
  transfers between devices with their start and end apart: 14, of which 9 were waited for; matrix products, arithmetic and copies ran while one was open for 4% of the time, Pallas kernels for 4%

profile of v2, /device:TPU:1, one launch (start us, length us, event | category | flops | bytes accessed | tf_op | source)
XLA Modules:
  0.0 150.8 jit_solution(12143691251292720594)
XLA Ops:
  0.6 0.0 copy-start
  0.6 7.0 %collective-permute-start = (bf16[512,256]{1,0:T(8,128)(2,1)}, bf16[512,256]{1,0:T(8,128)(2,1)S(1)}, u32[]{:S(2)}, u32[]{:S(2)}) collective-permute-start(bf16[512,256]{1,0:T(8,128)(2,1)} %param.5), channel_id=1, source_target_pairs={{0,0},{1,121},{2,130},{3,251},{4,260},{5,381},{6,390},{7,511},{8,8... | collective-permute-start | bytes 786440 | tf_op jit(solution)/shard_map/ppermute | solution.py:34
  7.6 6.1 %collective-permute-start.3 = (bf16[512,256]{1,0:T(8,128)(2,1)}, bf16[512,256]{1,0:T(8,128)(2,1)S(1)}, u32[]{:S(2)}, u32[]{:S(2)}) collective-permute-start(bf16[512,256]{1,0:T(8,128)(2,1)} %param.5), channel_id=1, source_target_pairs={{0,16},{1,105},{2,146},{3,235},{4,276},{5,365},{6,406},{7,495},{8,... | collective-permute-start | bytes 786440 | tf_op jit(solution)/shard_map/ppermute | solution.py:34
  13.8 0.0 collective-permute-done
  13.8 6.4 %collective-permute-start.1 = (bf16[512,256]{1,0:T(8,128)(2,1)S(1)}, bf16[512,256]{1,0:T(8,128)(2,1)S(1)}, u32[]{:S(2)}, u32[]{:S(2)}) collective-permute-start(bf16[512,256]{1,0:T(8,128)(2,1)S(1)} %collective-permute-done), channel_id=1, source_target_pairs={{0,8},{1,505},{2,10},{3,507},{4,12},{5,509},{6,14},{7,511},{8,16},... | collective-permute-start | bytes 786440 | tf_op jit(solution)/shard_map/ppermute | solution.py:34
  20.1 5.5 %collective-permute-done.3 = bf16[512,256]{1,0:T(8,128)(2,1)S(1)} collective-permute-done((bf16[512,256]{1,0:T(8,128)(2,1)}, bf16[512,256]{1,0:T(8,128)(2,1)S(1)}, u32[]{:S(2)}, u32[]{:S(2)}) %collective-permute-start.3) | collective-permute-done | bytes 262176 | tf_op jit(solution)/shard_map/ppermute | solution.py:34
  25.6 4.5 %collective-permute-start.4 = (bf16[512,256]{1,0:T(8,128)(2,1)S(1)}, bf16[512,256]{1,0:T(8,128)(2,1)S(1)}, u32[]{:S(2)}, u32[]{:S(2)}) collective-permute-start(bf16[512,256]{1,0:T(8,128)(2,1)S(1)} %collective-permute-done.3), channel_id=1, source_target_pairs={{0,8},{1,505},{2,10},{3,507},{4,12},{5,509},{6,14},{7,511},{8,16},... | collective-permute-start | bytes 786440 | tf_op jit(solution)/shard_map/ppermute | solution.py:34
  30.2 0.0 collective-permute-done.1
  30.2 1.9 %collective-permute-start.2 = (bf16[1024,256]{1,0:T(8,128)(2,1)S(1)}, bf16[1024,256]{1,0:T(8,128)(2,1)S(1)}, u32[]{:S(2)}, u32[]{:S(2)}) collective-permute-start(bf16[1024,256]{1,0:T(8,128)(2,1)S(1)} %constant_dynamic-update-slice_fusion.own0), channel_id=1, source_target_pairs={{0,65},{1,448},{2,67},{3,450},{4,69},{5,452},{6,71},{7,454},{8,73}... | collective-permute-start | bytes 1572872 | tf_op jit(solution)/shard_map/ppermute | solution.py:34
  32.1 1.3 collective-permute-done.4
  33.4 4.5 %collective-permute-start.5 = (bf16[1024,256]{1,0:T(8,128)(2,1)S(1)}, bf16[1024,256]{1,0:T(8,128)(2,1)S(1)}, u32[]{:S(2)}, u32[]{:S(2)}) collective-permute-start(bf16[1024,256]{1,0:T(8,128)(2,1)S(1)} %constant_dynamic-update-slice_fusion.2.own1), channel_id=1, source_target_pairs={{0,65},{1,448},{2,67},{3,450},{4,69},{5,452},{6,71},{7,454},{8,73}... | collective-permute-start | bytes 1572872 | tf_op jit(solution)/shard_map/ppermute | solution.py:34
  37.9 0.0 copy-start.4
  38.0 3.9 %shard_map.76.held = bf16[8,512,512]{2,1,0:T(8,128)(2,1)} custom-call(s32[1,8]{1,0:T(1,128)} %mask_ref.9, bf16[1,8,512,512]{3,2,1,0:T(8,128)(2,1)} %tiles_ref.1), custom_call_target="tpu_custom_call" | custom-call | tf_op jit(solution)/shard_map/pallas_call | solution.py:191
  41.8 0.0 copy-done
  41.9 2.9 %collective-permute-done.2.other0 = bf16[1024,256]{1,0:T(8,128)(2,1)S(1)} collective-permute-done((bf16[1024,256]{1,0:T(8,128)(2,1)S(1)}, bf16[1024,256]{1,0:T(8,128)(2,1)S(1)}, u32[]{:S(2)}, u32[]{:S(2)}) %collective-permute-start.2) | collective-permute-done | bytes 524320 | tf_op jit(solution)/shard_map/ppermute | solution.py:34
  44.8 0.0 copy-done.4
  44.8 0.0 copy-start.1
  44.8 2.2 %copy-done.1 = bf16[8,512,512]{2,1,0:T(8,128)(2,1)S(1)} copy-done((bf16[8,512,512]{2,1,0:T(8,128)(2,1)S(1)}, bf16[8,512,512]{2,1,0:T(8,128)(2,1)}, u32[]{:S(2)}) %copy-start.1) | copy-done | bytes 4194328
  47.0 0.9 shard_map.77.before
  47.9 0.0 copy-start.3
  47.9 0.0 copy-start.2
  47.9 2.5 %collective-permute-done.5.other1 = bf16[1024,256]{1,0:T(8,128)(2,1)S(1)} collective-permute-done((bf16[1024,256]{1,0:T(8,128)(2,1)S(1)}, bf16[1024,256]{1,0:T(8,128)(2,1)S(1)}, u32[]{:S(2)}, u32[]{:S(2)}) %collective-permute-start.5) | collective-permute-done | bytes 524320 | tf_op jit(solution)/shard_map/ppermute | solution.py:34
  50.4 0.6 shard_map.78
  51.0 2.2 %all-gather = f32[512,256]{1,0:T(8,128)S(1)} all-gather(f32[256,256]{1,0:T(8,128)S(1)} %get-tuple-element.12), channel_id=2, replica_groups=mesh['zl'=2,'x'=4,'y'=8,'zh'=4,'c'=2] {'c'}, dimensions={0}, use_global_device_ids=true | all-gather | bytes 786432 | tf_op jit(solution)/shard_map/all_gather | solution.py:222
  53.2 0.1 fusion.7
  53.3 20.4 %all-gather.1 = bf16[1024,256]{1,0:T(8,128)(2,1)S(1)} all-gather(bf16[256,256]{1,0:T(8,128)(2,1)S(1)} %fusion.7), channel_id=3, replica_groups=mesh['zl'=2,'x'=4,'y'=8,'zh'=4,'c'=2] {'zh'}, dimensions={0}, use_global_device_ids=true | all-gather | bytes 655360 | tf_op jit(solution)/shard_map/all_gather | solution.py:224
  73.7 0.0 copy-done.3
  73.7 0.6 shard_map.79
  74.3 3.0 %all-gather.2 = bf16[1280,256]{1,0:T(8,128)(2,1)S(1)} all-gather(bf16[640,256]{1,0:T(8,128)(2,1)S(1)} %shard_map.79), channel_id=4, replica_groups=mesh['zl'=2,'x'=4,'y'=8,'zh'=4,'c'=2] {'c'}, dimensions={0}, use_global_device_ids=true | all-gather | bytes 983040 | tf_op jit(solution)/shard_map/all_gather | solution.py:234
  77.3 0.0 copy-done.2
  77.3 1.0 shard_map.80
  78.3 2.2 %collective-permute-start.6 = (bf16[2,2,256,256]{3,2,1,0:T(8,128)(2,1)S(1)}, bf16[2,2,256,256]{3,2,1,0:T(8,128)(2,1)S(1)}, u32[]{:S(2)}, u32[]{:S(2)}) collective-permute-start(bf16[2,2,256,256]{3,2,1,0:T(8,128)(2,1)S(1)} %get-tuple-element.14), channel_id=1, source_target_pairs={{0,65},{1,448},{2,67},{3,450},{4,69},{5,452},{6,71},{7,454},{8,73}... | collective-permute-start | bytes 1572872 | tf_op jit(solution)/shard_map/ppermute | solution.py:34
  80.6 0.6 shard_map.81
  81.2 5.4 %collective-permute-start.9 = (bf16[2,2,256,256]{3,2,1,0:T(8,128)(2,1)S(1)}, bf16[2,2,256,256]{3,2,1,0:T(8,128)(2,1)S(1)}, u32[]{:S(2)}, u32[]{:S(2)}) collective-permute-start(bf16[2,2,256,256]{3,2,1,0:T(8,128)(2,1)S(1)} %shard_map.81), channel_id=1, source_target_pairs={{0,65},{1,448},{2,67},{3,450},{4,69},{5,452},{6,71},{7,454},{8,73}... | collective-permute-start | bytes 1572872 | tf_op jit(solution)/shard_map/ppermute | solution.py:34
  86.7 4.3 %collective-permute-done.6 = bf16[2,2,256,256]{3,2,1,0:T(8,128)(2,1)S(1)} collective-permute-done((bf16[2,2,256,256]{3,2,1,0:T(8,128)(2,1)S(1)}, bf16[2,2,256,256]{3,2,1,0:T(8,128)(2,1)S(1)}, u32[]{:S(2)}, u32[]{:S(2)}) %collective-permute-start.6) | collective-permute-done | bytes 524320 | tf_op jit(solution)/shard_map/ppermute | solution.py:34
  90.9 0.8 fusion.2
  91.7 1.9 %collective-permute-start.7 = (bf16[2,256,256]{2,1,0:T(8,128)(2,1)}, bf16[2,256,256]{2,1,0:T(8,128)(2,1)}, u32[]{:S(2)}, u32[]{:S(2)}) collective-permute-start(bf16[2,256,256]{2,1,0:T(8,128)(2,1)} %fusion.2), channel_id=1, source_target_pairs={{0,504},{1,9},{2,506},{3,11},{4,508},{5,13},{6,510},{7,15},{8,0},{... | collective-permute-start | bytes 786440 | tf_op jit(solution)/shard_map/ppermute | solution.py:34
  93.6 2.9 %collective-permute-done.9 = bf16[2,2,256,256]{3,2,1,0:T(8,128)(2,1)S(1)} collective-permute-done((bf16[2,2,256,256]{3,2,1,0:T(8,128)(2,1)S(1)}, bf16[2,2,256,256]{3,2,1,0:T(8,128)(2,1)S(1)}, u32[]{:S(2)}, u32[]{:S(2)}) %collective-permute-start.9) | collective-permute-done | bytes 524320 | tf_op jit(solution)/shard_map/ppermute | solution.py:34
  96.5 0.1 fusion.3
  96.6 1.9 %collective-permute-start.10 = (bf16[2,256,256]{2,1,0:T(8,128)(2,1)S(1)}, bf16[2,256,256]{2,1,0:T(8,128)(2,1)}, u32[]{:S(2)}, u32[]{:S(2)}) collective-permute-start(bf16[2,256,256]{2,1,0:T(8,128)(2,1)S(1)} %fusion.3), channel_id=1, source_target_pairs={{0,504},{1,9},{2,506},{3,11},{4,508},{5,13},{6,510},{7,15},{8,0},{... | collective-permute-start | bytes 786440 | tf_op jit(solution)/shard_map/ppermute | solution.py:34
  98.6 0.7 broadcast_in_dim.6
  99.3 4.5 %all-to-all-start = ((f32[8,32,256]{2,1,0:T(8,128)}), f32[8,32,256]{2,1,0:T(8,128)S(1)}, u32[]{:S(2)}, u32[]{:S(2)}) async-start(f32[8,32,256]{2,1,0:T(8,128)} %broadcast_in_dim.6), calls=%async_computation | async-start | bytes 524288 | tf_op jit(solution)/shard_map/all_to_all | solution.py:182
  103.7 0.0 collective-permute-done.7
  103.8 1.7 %fusion.1 = bf16[2,256,256]{2,1,0:T(8,128)(2,1)} fusion(bf16[2,256,256]{2,1,0:T(8,128)(2,1)} %collective-permute-done.7, bf16[2,2,256,256]{3,2,1,0:T(8,128)(2,1)S(1)} %collective-permute-done.6, bf16[2,2,256,256]{3,2,1,0:T(8,128)(2,1)S(1)} %get-tuple-element.13), kind=kLoop, calls=%fused_computation.3 | loop fusion | flops 786432 | bytes 1048576 | tf_op jit(solution)/shard_map/convert_element_type | solution.py:245
  105.5 2.0 %collective-permute-start.8 = (bf16[2,256,256]{2,1,0:T(8,128)(2,1)}, bf16[2,256,256]{2,1,0:T(8,128)(2,1)S(1)}, u32[]{:S(2)}, u32[]{:S(2)}) collective-permute-start(bf16[2,256,256]{2,1,0:T(8,128)(2,1)} %fusion.1), channel_id=1, source_target_pairs={{0,0},{1,393},{2,386},{3,267},{4,260},{5,141},{6,134},{7,15},{8,8}... | collective-permute-start | bytes 786440 | tf_op jit(solution)/shard_map/ppermute | solution.py:34
  107.5 0.6 collective-permute-done.10
  108.1 1.0 fusion
  109.1 9.9 %collective-permute-start.11 = (bf16[2,256,256]{2,1,0:T(8,128)(2,1)S(1)}, bf16[2,256,256]{2,1,0:T(8,128)(2,1)S(1)}, u32[]{:S(2)}, u32[]{:S(2)}) collective-permute-start(bf16[2,256,256]{2,1,0:T(8,128)(2,1)S(1)} %fusion), channel_id=1, source_target_pairs={{0,496},{1,409},{2,370},{3,283},{4,244},{5,157},{6,118},{7,31},{8,... | collective-permute-start | bytes 786440 | tf_op jit(solution)/shard_map/ppermute | solution.py:34
  119.0 0.7 slice.100
  119.7 0.0 all-to-all-done
  119.7 0.7 broadcast_in_dim.7
  120.5 3.5 %all-to-all-start.1 = ((f32[8,32,256]{2,1,0:T(8,128)}), f32[8,32,256]{2,1,0:T(8,128)S(1)}, u32[]{:S(2)}, u32[]{:S(2)}) async-start(f32[8,32,256]{2,1,0:T(8,128)} %broadcast_in_dim.7), calls=%async_computation.1 | async-start | bytes 524288 | tf_op jit(solution)/shard_map/all_to_all | solution.py:182
  124.0 0.0 collective-permute-done.8
  124.0 2.8 %collective-permute-done.11 = bf16[2,256,256]{2,1,0:T(8,128)(2,1)S(1)} collective-permute-done((bf16[2,256,256]{2,1,0:T(8,128)(2,1)S(1)}, bf16[2,256,256]{2,1,0:T(8,128)(2,1)S(1)}, u32[]{:S(2)}, u32[]{:S(2)}) %collective-permute-start.11) | collective-permute-done | bytes 262176 | tf_op jit(solution)/shard_map/ppermute | solution.py:34
  126.8 0.1 convert_add_fusion
  126.8 2.2 %all_gather.40 = f32[2,256,256]{2,1,0:T(8,128)S(1)} all-gather(f32[1,256,256]{2,1,0:T(8,128)S(1)} %convert_add_fusion), channel_id=1, replica_groups=mesh['zl'=2,'x'=4,'y'=8,'zh'=4,'c'=2] {'c'}, dimensions={0}, use_global_device_ids=true | all-gather | bytes 786432 | tf_op jit(solution)/shard_map/all_gather | solution.py:256
  129.0 0.1 fusion.8
  129.1 0.9 all-to-all-done.1
  130.1 16.1 %all-gather.3 = bf16[1152,256]{1,0:T(8,128)(2,1)S(1)} all-gather(bf16[288,256]{1,0:T(8,128)(2,1)S(1)} %pad_maximum_fusion), channel_id=5, replica_groups=mesh['zl'=2,'x'=4,'y'=8,'zh'=4,'c'=2] {'zh'}, dimensions={0}, use_global_device_ids=true | all-gather | bytes 737280 | tf_op jit(solution)/shard_map/all_gather | solution.py:258
  146.2 0.1 shard_map.82
  146.3 3.6 %all-gather.4 = bf16[768,256]{1,0:T(8,128)(2,1)S(1)} all-gather(bf16[384,256]{1,0:T(8,128)(2,1)S(1)} %shard_map.82), channel_id=6, replica_groups=mesh['zl'=2,'x'=4,'y'=8,'zh'=4,'c'=2] {'c'}, dimensions={0}, use_global_device_ids=true | all-gather | bytes 589824 | tf_op jit(solution)/shard_map/all_gather | solution.py:272
  149.9 0.8 shard_map.83
  (12 shorter events, 0.2 us)
Async XLA Ops:
  0.6 41.2 %copy-start = (bf16[512,256]{1,0:T(8,128)(2,1)S(1)}, bf16[512,256]{1,0:T(8,128)(2,1)}, u32[]{:S(2)}) copy-start(bf16[512,256]{1,0:T(8,128)(2,1)} %param.7) | copy-start | bytes 786436
  0.6 13.1 %collective-permute-start = (bf16[512,256]{1,0:T(8,128)(2,1)}, bf16[512,256]{1,0:T(8,128)(2,1)S(1)}, u32[]{:S(2)}, u32[]{:S(2)}) collective-permute-start(bf16[512,256]{1,0:T(8,128)(2,1)} %param.5), channel_id=1, source_target_pairs={{0,0},{1,121},{2,130},{3,251},{4,260},{5,381},{6,390},{7,511},{8,8... | collective-permute-start | bytes 786440 | tf_op jit(solution)/shard_map/ppermute | solution.py:34
  7.6 18.0 %collective-permute-start.3 = (bf16[512,256]{1,0:T(8,128)(2,1)}, bf16[512,256]{1,0:T(8,128)(2,1)S(1)}, u32[]{:S(2)}, u32[]{:S(2)}) collective-permute-start(bf16[512,256]{1,0:T(8,128)(2,1)} %param.5), channel_id=1, source_target_pairs={{0,16},{1,105},{2,146},{3,235},{4,276},{5,365},{6,406},{7,495},{8,... | collective-permute-start | bytes 786440 | tf_op jit(solution)/shard_map/ppermute | solution.py:34
  13.8 16.4 %collective-permute-start.1 = (bf16[512,256]{1,0:T(8,128)(2,1)S(1)}, bf16[512,256]{1,0:T(8,128)(2,1)S(1)}, u32[]{:S(2)}, u32[]{:S(2)}) collective-permute-start(bf16[512,256]{1,0:T(8,128)(2,1)S(1)} %collective-permute-done), channel_id=1, source_target_pairs={{0,8},{1,505},{2,10},{3,507},{4,12},{5,509},{6,14},{7,511},{8,16},... | collective-permute-start | bytes 786440 | tf_op jit(solution)/shard_map/ppermute | solution.py:34
  25.6 7.8 %collective-permute-start.4 = (bf16[512,256]{1,0:T(8,128)(2,1)S(1)}, bf16[512,256]{1,0:T(8,128)(2,1)S(1)}, u32[]{:S(2)}, u32[]{:S(2)}) collective-permute-start(bf16[512,256]{1,0:T(8,128)(2,1)S(1)} %collective-permute-done.3), channel_id=1, source_target_pairs={{0,8},{1,505},{2,10},{3,507},{4,12},{5,509},{6,14},{7,511},{8,16},... | collective-permute-start | bytes 786440 | tf_op jit(solution)/shard_map/ppermute | solution.py:34
  30.2 14.6 %collective-permute-start.2 = (bf16[1024,256]{1,0:T(8,128)(2,1)S(1)}, bf16[1024,256]{1,0:T(8,128)(2,1)S(1)}, u32[]{:S(2)}, u32[]{:S(2)}) collective-permute-start(bf16[1024,256]{1,0:T(8,128)(2,1)S(1)} %constant_dynamic-update-slice_fusion.own0), channel_id=1, source_target_pairs={{0,65},{1,448},{2,67},{3,450},{4,69},{5,452},{6,71},{7,454},{8,73}... | collective-permute-start | bytes 1572872 | tf_op jit(solution)/shard_map/ppermute | solution.py:34
  33.4 16.9 %collective-permute-start.5 = (bf16[1024,256]{1,0:T(8,128)(2,1)S(1)}, bf16[1024,256]{1,0:T(8,128)(2,1)S(1)}, u32[]{:S(2)}, u32[]{:S(2)}) collective-permute-start(bf16[1024,256]{1,0:T(8,128)(2,1)S(1)} %constant_dynamic-update-slice_fusion.2.own1), channel_id=1, source_target_pairs={{0,65},{1,448},{2,67},{3,450},{4,69},{5,452},{6,71},{7,454},{8,73}... | collective-permute-start | bytes 1572872 | tf_op jit(solution)/shard_map/ppermute | solution.py:34
  37.9 6.8 %copy-start.4 = (s32[1,8]{1,0:T(1,128)S(1)}, s32[1,8]{1,0:T(1,128)}, u32[]{:S(2)}) copy-start(s32[1,8]{1,0:T(1,128)} %mask_ref.9) | copy-start | bytes 100
  44.8 2.2 %copy-start.1 = (bf16[8,512,512]{2,1,0:T(8,128)(2,1)S(1)}, bf16[8,512,512]{2,1,0:T(8,128)(2,1)}, u32[]{:S(2)}) copy-start(bf16[8,512,512]{2,1,0:T(8,128)(2,1)} %shard_map.76.held) | copy-start | bytes 12582916
  47.9 25.8 %copy-start.3 = (bf16[256,256]{1,0:T(8,128)(2,1)S(1)}, bf16[256,256]{1,0:T(8,128)(2,1)}, u32[]{:S(2)}) copy-start(bf16[256,256]{1,0:T(8,128)(2,1)} %weight_ref.1) | copy-start | bytes 393220
  47.9 29.4 %copy-start.2 = (bf16[8,512,512]{2,1,0:T(8,128)(2,1)S(1)}, bf16[8,512,512]{2,1,0:T(8,128)(2,1)}, u32[]{:S(2)}) copy-start(bf16[8,512,512]{2,1,0:T(8,128)(2,1)} %shard_map.76.held) | copy-start | bytes 12582916
  78.3 12.6 %collective-permute-start.6 = (bf16[2,2,256,256]{3,2,1,0:T(8,128)(2,1)S(1)}, bf16[2,2,256,256]{3,2,1,0:T(8,128)(2,1)S(1)}, u32[]{:S(2)}, u32[]{:S(2)}) collective-permute-start(bf16[2,2,256,256]{3,2,1,0:T(8,128)(2,1)S(1)} %get-tuple-element.14), channel_id=1, source_target_pairs={{0,65},{1,448},{2,67},{3,450},{4,69},{5,452},{6,71},{7,454},{8,73}... | collective-permute-start | bytes 1572872 | tf_op jit(solution)/shard_map/ppermute | solution.py:34
  81.2 15.4 %collective-permute-start.9 = (bf16[2,2,256,256]{3,2,1,0:T(8,128)(2,1)S(1)}, bf16[2,2,256,256]{3,2,1,0:T(8,128)(2,1)S(1)}, u32[]{:S(2)}, u32[]{:S(2)}) collective-permute-start(bf16[2,2,256,256]{3,2,1,0:T(8,128)(2,1)S(1)} %shard_map.81), channel_id=1, source_target_pairs={{0,65},{1,448},{2,67},{3,450},{4,69},{5,452},{6,71},{7,454},{8,73}... | collective-permute-start | bytes 1572872 | tf_op jit(solution)/shard_map/ppermute | solution.py:34
  91.7 12.1 %collective-permute-start.7 = (bf16[2,256,256]{2,1,0:T(8,128)(2,1)}, bf16[2,256,256]{2,1,0:T(8,128)(2,1)}, u32[]{:S(2)}, u32[]{:S(2)}) collective-permute-start(bf16[2,256,256]{2,1,0:T(8,128)(2,1)} %fusion.2), channel_id=1, source_target_pairs={{0,504},{1,9},{2,506},{3,11},{4,508},{5,13},{6,510},{7,15},{8,0},{... | collective-permute-start | bytes 786440 | tf_op jit(solution)/shard_map/ppermute | solution.py:34
  96.6 11.4 %collective-permute-start.10 = (bf16[2,256,256]{2,1,0:T(8,128)(2,1)S(1)}, bf16[2,256,256]{2,1,0:T(8,128)(2,1)}, u32[]{:S(2)}, u32[]{:S(2)}) collective-permute-start(bf16[2,256,256]{2,1,0:T(8,128)(2,1)S(1)} %fusion.3), channel_id=1, source_target_pairs={{0,504},{1,9},{2,506},{3,11},{4,508},{5,13},{6,510},{7,15},{8,0},{... | collective-permute-start | bytes 786440 | tf_op jit(solution)/shard_map/ppermute | solution.py:34
  99.3 20.4 %all-to-all-start = ((f32[8,32,256]{2,1,0:T(8,128)}), f32[8,32,256]{2,1,0:T(8,128)S(1)}, u32[]{:S(2)}, u32[]{:S(2)}) async-start(f32[8,32,256]{2,1,0:T(8,128)} %broadcast_in_dim.6), calls=%async_computation | async-start | bytes 524288 | tf_op jit(solution)/shard_map/all_to_all | solution.py:182
  105.5 18.5 %collective-permute-start.8 = (bf16[2,256,256]{2,1,0:T(8,128)(2,1)}, bf16[2,256,256]{2,1,0:T(8,128)(2,1)S(1)}, u32[]{:S(2)}, u32[]{:S(2)}) collective-permute-start(bf16[2,256,256]{2,1,0:T(8,128)(2,1)} %fusion.1), channel_id=1, source_target_pairs={{0,0},{1,393},{2,386},{3,267},{4,260},{5,141},{6,134},{7,15},{8,8}... | collective-permute-start | bytes 786440 | tf_op jit(solution)/shard_map/ppermute | solution.py:34
  109.1 17.7 %collective-permute-start.11 = (bf16[2,256,256]{2,1,0:T(8,128)(2,1)S(1)}, bf16[2,256,256]{2,1,0:T(8,128)(2,1)S(1)}, u32[]{:S(2)}, u32[]{:S(2)}) collective-permute-start(bf16[2,256,256]{2,1,0:T(8,128)(2,1)S(1)} %fusion), channel_id=1, source_target_pairs={{0,496},{1,409},{2,370},{3,283},{4,244},{5,157},{6,118},{7,31},{8,... | collective-permute-start | bytes 786440 | tf_op jit(solution)/shard_map/ppermute | solution.py:34
  120.5 9.6 %all-to-all-start.1 = ((f32[8,32,256]{2,1,0:T(8,128)}), f32[8,32,256]{2,1,0:T(8,128)S(1)}, u32[]{:S(2)}, u32[]{:S(2)}) async-start(f32[8,32,256]{2,1,0:T(8,128)} %broadcast_in_dim.7), calls=%async_computation.1 | async-start | bytes 524288 | tf_op jit(solution)/shard_map/all_to_all | solution.py:182

commit v3 on v2

--- a/solution.py
+++ b/solution.py
@@ -22,7 +22,6 @@
 VMEM = pl.BlockSpec(memory_space=pltpu.VMEM)
 HBM = pl.BlockSpec(memory_space=pltpu.HBM)
 PARAMS = pltpu.CompilerParams(vmem_limit_bytes=24 * 1024 * 1024)
-WIDE_PARAMS = pltpu.CompilerParams(vmem_limit_bytes=60 * 1024 * 1024)
 
 
 def route(value, target):
@@ -42,6 +41,11 @@
     return route(value, partner)
 
 
+def cross_back(i, r):
+    i2, r2 = partner(i, r)
+    return (i2 - side(r2), r2)
+
+
 def side(r):
     return 1 - 2 * (r % 2)
 
@@ -50,31 +54,25 @@
     return (7 * core, 1 + 5 * core, 2 + 3 * core, 3 + core)[2 * pair + slot]
 
 
-def load_kernel(mask_ref, tiles_ref, held_ref, sems):
-    def copy(t):
-        return pltpu.make_async_copy(tiles_ref.at[0, t], held_ref.at[t], sems.at[t])
-
-    for t in range(8):
+def tile_steps(core_ref, mask_ref, tiles_ref, held, sems, work, present, absent):
+    core = core_ref[0]
+    offsets = [offsets_of(core if member == 0 else 1 - core, pair, slot) for member, pair, slot in work]
+
+    def copy(step, t):
+        return pltpu.make_async_copy(tiles_ref.at[0, t], held.at[step], sems.at[step])
+
+    for step, t in enumerate(offsets):
 
         @pl.when(mask_ref[0, t] > 0)
         def _():
-            copy(t).start()
-
-    for t in range(8):
+            copy(step, t).start()
+
+    for step, t in enumerate(offsets):
 
         @pl.when(mask_ref[0, t] > 0)
         def _():
-            copy(t).wait()
-
-
-def tile_steps(core_ref, mask_ref, held, work, present, absent):
-    core = core_ref[0]
-    for step, (member, pair, slot) in enumerate(work):
-        t = offsets_of(core if member == 0 else 1 - core, pair, slot)
-
-        @pl.when(mask_ref[0, t] > 0)
-        def _():
-            present(step, held.at[t])
+            copy(step, t).wait()
+            present(step, held.at[step])
 
         if absent is not None:
 
@@ -83,28 +81,33 @@
                 absent(step)
 
 
-def early_kernel(core_ref, mask_ref, held, own0, other0, own1, acc):
-    blocks = (own0, other0, own1)
+def tile_scratch(count):
+    return [pltpu.VMEM((count, ROWS, ROWS), BF16), pltpu.SemaphoreType.DMA((count,))]
+
+
+def early_kernel(core_ref, mask_ref, tiles_ref, near, near_d, near_e, near_r, far, acc, held, sems):
     acc[...] = jnp.zeros_like(acc)
+    sources = ((near, 0 * ROWS), (near_d, 0 * ROWS), (near_e, 0 * ROWS), (near_r, 0 * ROWS), (far, 0 * ROWS),)
 
     def present(step, tile):
-        start = (step % 2) * ROWS
-        acc[...] += jnp.dot(tile[...], blocks[step // 2][start : start + ROWS, :], preferred_element_type=F32)
-
-    work = [(member, pair, slot) for member, pair in ((0, 0), (1, 0), (0, 1)) for slot in range(2)]
-    tile_steps(core_ref, mask_ref, held, work, present, None)
-
-
-def late_kernel(core_ref, mask_ref, held, before, other1, keep_ref, send_ref, acc):
+        block, start = sources[step]
+        acc[...] += jnp.dot(tile[...], block[start : start + ROWS, :], preferred_element_type=F32)
+
+    tile_steps(core_ref, mask_ref, tiles_ref, held, sems, [(0, 0, 0), (1, 0, 1), (1, 0, 0), (0, 0, 1), (0, 1, 0)], present, None)
+
+
+def late_kernel(core_ref, mask_ref, tiles_ref, before, far_d, far_e, far_r, keep_ref, send_ref, acc, held, sems):
     core = core_ref[0]
     acc[...] = before[...]
+    sources = ((far_d, 0 * ROWS), (far_e, 0 * ROWS), (far_r, 0 * ROWS),)
 
     def present(step, tile):
-        acc[...] += jnp.dot(tile[...], other1[step * ROWS : (step + 1) * ROWS, :], preferred_element_type=F32)
-
-    tile_steps(core_ref, mask_ref, held, [(1, 1, 0), (1, 1, 1)], present, None)
+        block, start = sources[step]
+        acc[...] += jnp.dot(tile[...], block[start : start + ROWS, :], preferred_element_type=F32)
+
+    tile_steps(core_ref, mask_ref, tiles_ref, held, sems, [(1, 1, 1), (1, 1, 0), (0, 1, 1)], present, None)
     keep_ref[...] = acc[pl.ds(pl.multiple_of(core * HALF, HALF), HALF), :]
-    send_ref[...] = acc[pl.ds(pl.multiple_of(HALF - core * HALF, HALF), HALF), :]
+    send_ref[...] = acc[pl.ds(pl.multiple_of(HALF - core * HALF, HALF), HALF), :].astype(send_ref.dtype)
 
 
 def middle_kernel(zh_ref, parts_ref, weight_ref, grad_ref, pack_ref, full):
@@ -127,7 +130,9 @@
     pack_ref[576:640] = (term - term_high.astype(F32)).astype(BF16)
 
 
-def backward_kernel(plan, core_ref, mask_ref, held, pack_ref, *outs):
+def backward_kernel(plan, core_ref, mask_ref, tiles_ref, pack_ref, *rest):
+    outs, held, sems = rest[: len(plan)], rest[-2], rest[-1]
+
     def present(step, tile):
         value = jnp.dot(pack_ref[0, HALF : 2 * HALF], tile[:HALF, :], preferred_element_type=F32)
         value = value + jnp.dot(pack_ref[1, HALF : 2 * HALF], tile[HALF:, :], preferred_element_type=F32)
@@ -138,8 +143,8 @@
     def absent(step):
         outs[step // 2][step % 2] = jnp.zeros((2, HIDDEN, HALF), BF16)
 
-    work = [(member, pair, slot) for member, pair in plan for slot in range(2)]
-    tile_steps(core_ref, mask_ref, held, work, present, absent)
+    work = [(member, pair, slot) for member, slot in plan for pair in range(2)]
+    tile_steps(core_ref, mask_ref, tiles_ref, held, sems, work, present, absent)
 
 
 def turn_kernel(parts_ref, out_ref):
@@ -159,15 +164,16 @@
             weight_ref[64 * s + 32 * c : 64 * s + 32 * c + 32] = packs_ref[c, start : start + 32].astype(F32)
 
 
-def products(plan, core, mask, held, packs):
+def products(plan, core, mask, tiles, packs):
     return pl.pallas_call(
         functools.partial(backward_kernel, plan),
         out_shape=[jax.ShapeDtypeStruct((2, 2, HIDDEN, HALF), BF16) for _ in plan],
-        in_specs=[SMEM, SMEM, VMEM, VMEM],
+        in_specs=[SMEM, SMEM, HBM, VMEM],
         out_specs=[VMEM] * len(plan),
+        scratch_shapes=tile_scratch(2 * len(plan)),
         compiler_params=PARAMS,
         cost_estimate=pl.CostEstimate(flops=2 * 10**9, bytes_accessed=6 * 2**20, transcendentals=0),
-    )(core, mask, held, packs)
+    )(core, mask, tiles, packs)
 
 
 def total_of(*values):
@@ -187,38 +193,35 @@
     core = core_index.astype(jnp.int32).reshape(1)
     zh = lax.axis_index("zh").astype(jnp.int32).reshape(1)
     even = core_index == 0
-
-    held = pl.pallas_call(
-        load_kernel,
-        out_shape=jax.ShapeDtypeStruct((8, ROWS, ROWS), BF16),
-        in_specs=[SMEM, HBM],
-        out_specs=VMEM,
-        scratch_shapes=[pltpu.SemaphoreType.DMA((8,))],
-        compiler_params=WIDE_PARAMS,
-    )(tile_mask, tiles)
+    tiles = pltpu.with_memory_space_constraint(tiles, pltpu.HBM)
+
     fetched1 = route(features, lambda i, r: (i + 8 * r + 2 + 3 * (r % 2), r))
     fetched0 = route(features, lambda i, r: (i + 8 * r + 7 * (r % 2), r))
-    own0 = jnp.concatenate([fetched0, route(fetched0, lambda i, r: (i + side(r), r))])
-    own1 = jnp.concatenate([fetched1, route(fetched1, lambda i, r: (i + side(r), r))])
-    other0 = swap_pair(own0)
-    other1 = swap_pair(own1)
+    near_r = route(fetched0, lambda i, r: (i + side(r), r))
+    near_e = swap_pair(fetched0)
+    near_d = route(fetched0, lambda i, r: partner(i + side(r), r))
+    far_r = route(fetched1, lambda i, r: (i + side(r), r))
+    far_e = swap_pair(fetched1)
+    far_d = route(fetched1, lambda i, r: partner(i + side(r), r))
     half = jax.ShapeDtypeStruct((HALF, HIDDEN), F32)
+    half16 = jax.ShapeDtypeStruct((HALF, HIDDEN), BF16)
     before = pl.pallas_call(
         early_kernel,
         out_shape=jax.ShapeDtypeStruct((ROWS, HIDDEN), F32),
-        in_specs=[SMEM, SMEM] + [VMEM] * 4,
+        in_specs=[SMEM, SMEM, HBM] + [VMEM] * 5,
         out_specs=VMEM,
+        scratch_shapes=tile_scratch(5),
         compiler_params=PARAMS,
         cost_estimate=pl.CostEstimate(flops=2 * 10**9, bytes_accessed=6 * 2**20, transcendentals=0),
-    )(core, tile_mask, held, own0, other0, own1)
+    )(core, tile_mask, tiles, fetched0, near_d, near_e, near_r, fetched1)
     keep, send = pl.pallas_call(
         late_kernel,
-        out_shape=[half, half],
-        in_specs=[SMEM, SMEM] + [VMEM] * 3,
+        out_shape=[half, half16],
+        in_specs=[SMEM, SMEM, HBM] + [VMEM] * 4,
         out_specs=[VMEM, VMEM],
-        scratch_shapes=[pltpu.VMEM((ROWS, HIDDEN), F32)],
-        compiler_params=PARAMS,
-    )(core, tile_mask, held, before, other1)
+        scratch_shapes=[pltpu.VMEM((ROWS, HIDDEN), F32)] + tile_scratch(3),
+        compiler_params=PARAMS,
+    )(core, tile_mask, tiles, before, far_d, far_e, far_r)
     sent = lax.all_gather(send, "c")
     chip = (keep + jnp.where(even, sent[1], sent[0])).astype(BF16)
     parts = lax.all_gather(chip, "zh")
@@ -234,16 +237,14 @@
     packs = lax.all_gather(pack, "c")
     activated = packs[:, :HALF].reshape(ROWS, HIDDEN)
 
-    (send1,) = products(((1, 1),), core, tile_mask, held, packs)
-    got1 = swap_pair(send1)
-    send0, mine0, mine1 = products(((1, 0), (0, 0), (0, 1)), core, tile_mask, held, packs)
-    got0 = swap_pair(send0)
-    back1 = route(total_of(mine1[1], got1[1]).astype(BF16), lambda i, r: (i - side(r), r))
-    back0 = route(total_of(mine0[1], got0[1]).astype(BF16), lambda i, r: (i - side(r), r))
-    far = total_of(mine1[0], got1[0], back1).astype(BF16)
+    aside, other, across, own = products(((0, 1), (1, 0), (1, 1), (0, 0)), core, tile_mask, tiles, packs)
+    aside = route(aside, lambda i, r: (i - side(r), r))
+    other = swap_pair(other)
+    across = route(across, cross_back)
+    near = total_of(own[0], aside[0], other[0], across[0]).astype(BF16)
+    far = total_of(own[1], aside[1], other[1], across[1]).astype(BF16)
+    home_near = route(near, lambda i, r: (i - 8 * r - 7 * (r % 2), r))
     home_far = route(far, lambda i, r: (i - 8 * r - 2 - 3 * (r % 2), r))
-    near = total_of(mine0[0], got0[0], back0).astype(BF16)
-    home_near = route(near, lambda i, r: (i - 8 * r - 7 * (r % 2), r))
 
     high, low = packs[:, 512:576].astype(F32), packs[:, 576:640].astype(F32)
     term = lax.dynamic_slice_in_dim(high[0] + low[0] + (high[1] + low[1]), core_index * 32, 32, 0)
@@ -251,7 +252,9 @@
     term, _ = lax.optimization_barrier((term, far))
     term = (spread_sum(term, ("zl", "x")) * (BLOCKS * ROWS) ** -0.5).astype(BF16)
 
-    flipped = total_of(jnp.where(even, home_near[1], home_near[0]), jnp.where(even, home_far[1], home_far[0]))
+    flipped = total_of(
+        jnp.where(even, home_near[1], home_near[0]), jnp.where(even, home_far[1], home_far[0])
+    ).astype(BF16)
     kept = total_of(jnp.where(even, home_near[0], home_near[1]), jnp.where(even, home_far[0], home_far[1]))
     crossed = lax.all_gather(flipped, "c")
     chip_grad = (kept + jnp.where(even, crossed[1], crossed[0])).astype(BF16)

time: 152 us -> 151 us (level)
  blocking collectives: 47.5 us -> 52.4 us
  Pallas kernels: 8.52 us -> 3.7 us
  starting transfers between devices: 61.7 us -> 66.3 us
  other arithmetic: 3.96 us -> 1.92 us
  local copies, waits for them, and re-layouts: 4.5 us -> 2.88 us
    pallas_call x2 -> x1, Pallas kernels: 4.48 us -> 0.65 us  [shards(): pl.pallas_call(late_kernel, out_shape=[half, half16], in_specs=[SMEM, SME...]
    convert_element_type x4 -> x1, other arithmetic: 3.63 us -> 0.07 us  [shards(): flipped = total_of(jnp.where(even, home_near[1], home_near[0]), jnp.where...]
    ppermute x12 -> x13, starting transfers between devices: 53.7 us -> 56.6 us  [route(): return lax.ppermute(value, AXES, pairs)]
    all_gather x1, blocking collectives: 20.4 us -> 23.1 us  [shards(): parts = lax.all_gather(chip, 'zh')]
    all_gather x1, blocking collectives: 16.1 us -> 18.5 us  [shards(): grad_parts = lax.all_gather(jnp.concatenate([chip_grad, term]), 'zh')]
    all_to_all x2, starting transfers between devices: 7.96 us -> 9.71 us  [spread_sum(): return jnp.sum(lax.all_to_all(copies, axes, 0, 0), axis=0)]
    unnamed x12 -> x8, local copies, waits for them, and re-layouts: 2.25 us -> 0.67 us
    add x1, other arithmetic: 0.06 us -> 1.6 us  [total_of(): wide = wide + value.astype(F32)]
  transfers between devices with their start and end apart: 14 -> 15, of which waited for: 9 -> 5; matrix products, arithmetic and copies ran while one was open for 4% -> 3% of each run, Pallas kernels for 4% -> 0%
where the time goes in v3:
time: 151 us
  starting transfers between devices  66.3 us (44%)
  blocking collectives  52.4 us (35%)
  waiting for transfers between devices  23.1 us (15%)
  Pallas kernels  3.7 us (2%)
  local copies, waits for them, and re-layouts  2.88 us (2%)
  other arithmetic  1.92 us (1%)
    ppermute x13, starting transfers between devices, route(): return lax.ppermute(value, AXES, pairs)  56.6 us
    ppermute x13, waiting for transfers between devices, route(): return lax.ppermute(value, AXES, pairs)  23.1 us
    all_gather x1, blocking collectives, shards(): parts = lax.all_gather(chip, 'zh')  23.1 us
    all_gather x1, blocking collectives, shards(): grad_parts = lax.all_gather(jnp.concatenate([chip_grad, term]), 'zh')  18.5 us
    all_to_all x2, starting transfers between devices, spread_sum(): return jnp.sum(lax.all_to_all(copies, axes, 0, 0), axis=0)  9.71 us
    all_gather x1, blocking collectives, shards(): sent = lax.all_gather(send, 'c')  3.07 us
  transfers between devices with their start and end apart: 15, of which 5 were waited for; matrix products, arithmetic and copies ran while one was open for 3% of the time, Pallas kernels for 0%

profile of v3, /device:TPU:1, one launch (start us, length us, event | category | flops | bytes accessed | tf_op | source)
XLA Modules:
  0.0 151.2 jit_solution(9262905908401885969)
XLA Ops:
  0.6 0.0 copy-start
  0.6 7.0 %collective-permute-start = (bf16[512,256]{1,0:T(8,128)(2,1)}, bf16[512,256]{1,0:T(8,128)(2,1)S(1)}, u32[]{:S(2)}, u32[]{:S(2)}) collective-permute-start(bf16[512,256]{1,0:T(8,128)(2,1)} %param.5), channel_id=1, source_target_pairs={{0,0},{1,121},{2,130},{3,251},{4,260},{5,381},{6,390},{7,511},{8,8... | collective-permute-start | bytes 786440 | tf_op jit(solution)/shard_map/ppermute | solution.py:33
  7.6 6.1 %collective-permute-start.4 = (bf16[512,256]{1,0:T(8,128)(2,1)}, bf16[512,256]{1,0:T(8,128)(2,1)S(1)}, u32[]{:S(2)}, u32[]{:S(2)}) collective-permute-start(bf16[512,256]{1,0:T(8,128)(2,1)} %param.5), channel_id=1, source_target_pairs={{0,16},{1,105},{2,146},{3,235},{4,276},{5,365},{6,406},{7,495},{8,... | collective-permute-start | bytes 786440 | tf_op jit(solution)/shard_map/ppermute | solution.py:33
  13.8 0.0 collective-permute-done.near
  13.8 6.4 %collective-permute-start.3 = (bf16[512,256]{1,0:T(8,128)(2,1)S(1)}, bf16[512,256]{1,0:T(8,128)(2,1)S(1)}, u32[]{:S(2)}, u32[]{:S(2)}) collective-permute-start(bf16[512,256]{1,0:T(8,128)(2,1)S(1)} %collective-permute-done.near), channel_id=1, source_target_pairs={{0,8},{1,505},{2,10},{3,507},{4,12},{5,509},{6,14},{7,511},{8,16},... | collective-permute-start | bytes 786440 | tf_op jit(solution)/shard_map/ppermute | solution.py:33
  20.1 1.9 %collective-permute-start.2 = (bf16[512,256]{1,0:T(8,128)(2,1)S(1)}, bf16[512,256]{1,0:T(8,128)(2,1)S(1)}, u32[]{:S(2)}, u32[]{:S(2)}) collective-permute-start(bf16[512,256]{1,0:T(8,128)(2,1)S(1)} %collective-permute-done.near), channel_id=1, source_target_pairs={{0,65},{1,448},{2,67},{3,450},{4,69},{5,452},{6,71},{7,454},{8,73}... | collective-permute-start | bytes 786440 | tf_op jit(solution)/shard_map/ppermute | solution.py:33
  22.1 4.7 %collective-permute-start.1 = (bf16[512,256]{1,0:T(8,128)(2,1)S(1)}, bf16[512,256]{1,0:T(8,128)(2,1)S(1)}, u32[]{:S(2)}, u32[]{:S(2)}) collective-permute-start(bf16[512,256]{1,0:T(8,128)(2,1)S(1)} %collective-permute-done.near), channel_id=1, source_target_pairs={{0,73},{1,440},{2,75},{3,442},{4,77},{5,444},{6,79},{7,446},{8,81}... | collective-permute-start | bytes 786440 | tf_op jit(solution)/shard_map/ppermute | solution.py:33
  26.8 0.0 collective-permute-done.4.far
  26.8 3.4 %collective-permute-start.7 = (bf16[512,256]{1,0:T(8,128)(2,1)S(1)}, bf16[512,256]{1,0:T(8,128)(2,1)S(1)}, u32[]{:S(2)}, u32[]{:S(2)}) collective-permute-start(bf16[512,256]{1,0:T(8,128)(2,1)S(1)} %collective-permute-done.4.far), channel_id=1, source_target_pairs={{0,8},{1,505},{2,10},{3,507},{4,12},{5,509},{6,14},{7,511},{8,16},... | collective-permute-start | bytes 786440 | tf_op jit(solution)/shard_map/ppermute | solution.py:33
  30.2 1.9 %collective-permute-start.6 = (bf16[512,256]{1,0:T(8,128)(2,1)S(1)}, bf16[512,256]{1,0:T(8,128)(2,1)S(1)}, u32[]{:S(2)}, u32[]{:S(2)}) collective-permute-start(bf16[512,256]{1,0:T(8,128)(2,1)S(1)} %collective-permute-done.4.far), channel_id=1, source_target_pairs={{0,65},{1,448},{2,67},{3,450},{4,69},{5,452},{6,71},{7,454},{8,73}... | collective-permute-start | bytes 786440 | tf_op jit(solution)/shard_map/ppermute | solution.py:33
  32.1 0.0 collective-permute-done.3.near_r
  32.1 5.1 %collective-permute-start.5 = (bf16[512,256]{1,0:T(8,128)(2,1)S(1)}, bf16[512,256]{1,0:T(8,128)(2,1)S(1)}, u32[]{:S(2)}, u32[]{:S(2)}) collective-permute-start(bf16[512,256]{1,0:T(8,128)(2,1)S(1)} %collective-permute-done.4.far), channel_id=1, source_target_pairs={{0,73},{1,440},{2,75},{3,442},{4,77},{5,444},{6,79},{7,446},{8,81}... | collective-permute-start | bytes 786440 | tf_op jit(solution)/shard_map/ppermute | solution.py:33
  37.2 0.0 copy-done
  37.2 0.0 collective-permute-done.2.near_e
  37.2 0.0 collective-permute-done.1.near_d
  37.3 0.0 copy-start.2
  37.3 0.6 copy-done.2
  37.9 0.7 shard_map.76.before
  38.6 0.0 copy-start.1
  38.6 0.0 copy-start.3
  38.6 0.0 collective-permute-done.7.far_r
  38.6 3.8 %collective-permute-done.6.far_e = bf16[512,256]{1,0:T(8,128)(2,1)S(1)} collective-permute-done((bf16[512,256]{1,0:T(8,128)(2,1)S(1)}, bf16[512,256]{1,0:T(8,128)(2,1)S(1)}, u32[]{:S(2)}, u32[]{:S(2)}) %collective-permute-start.6) | collective-permute-done | bytes 262176 | tf_op jit(solution)/shard_map/ppermute | solution.py:33
  42.4 2.4 %collective-permute-done.5.far_d = bf16[512,256]{1,0:T(8,128)(2,1)S(1)} collective-permute-done((bf16[512,256]{1,0:T(8,128)(2,1)S(1)}, bf16[512,256]{1,0:T(8,128)(2,1)S(1)}, u32[]{:S(2)}, u32[]{:S(2)}) %collective-permute-start.5) | collective-permute-done | bytes 262176 | tf_op jit(solution)/shard_map/ppermute | solution.py:33
  44.8 0.7 shard_map.77
  45.4 3.1 %all-gather = bf16[512,256]{1,0:T(8,128)(2,1)S(1)} all-gather(bf16[256,256]{1,0:T(8,128)(2,1)S(1)} %get-tuple-element.13), channel_id=2, replica_groups=mesh['zl'=2,'x'=4,'y'=8,'zh'=4,'c'=2] {'c'}, dimensions={0}, use_global_device_ids=true | all-gather | bytes 393216 | tf_op jit(solution)/shard_map/all_gather | solution.py:225
  48.5 23.1 %all-gather.1 = bf16[1024,256]{1,0:T(8,128)(2,1)S(1)} all-gather(bf16[256,256]{1,0:T(8,128)(2,1)S(1)} %fusion.2), channel_id=3, replica_groups=mesh['zl'=2,'x'=4,'y'=8,'zh'=4,'c'=2] {'zh'}, dimensions={0}, use_global_device_ids=true | all-gather | bytes 655360 | tf_op jit(solution)/shard_map/all_gather | solution.py:227
  71.6 0.0 copy-done.1
  71.6 0.6 shard_map.78
  72.2 2.9 %all-gather.2 = bf16[1280,256]{1,0:T(8,128)(2,1)S(1)} all-gather(bf16[640,256]{1,0:T(8,128)(2,1)S(1)} %shard_map.78), channel_id=4, replica_groups=mesh['zl'=2,'x'=4,'y'=8,'zh'=4,'c'=2] {'c'}, dimensions={0}, use_global_device_ids=true | all-gather | bytes 983040 | tf_op jit(solution)/shard_map/all_gather | solution.py:237
  75.1 0.0 copy-done.3
  75.1 0.9 shard_map.79
  76.0 1.9 %collective-permute-start.8 = (bf16[2,2,256,256]{3,2,1,0:T(8,128)(2,1)S(1)}, bf16[2,2,256,256]{3,2,1,0:T(8,128)(2,1)}, u32[]{:S(2)}, u32[]{:S(2)}) collective-permute-start(bf16[2,2,256,256]{3,2,1,0:T(8,128)(2,1)S(1)} %get-tuple-element.15), channel_id=1, source_target_pairs={{0,504},{1,9},{2,506},{3,11},{4,508},{5,13},{6,510},{7,15},{8,0},{... | collective-permute-start | bytes 1572872 | tf_op jit(solution)/shard_map/ppermute | solution.py:33
  77.9 7.6 %collective-permute-start.9 = (bf16[2,2,256,256]{3,2,1,0:T(8,128)(2,1)S(1)}, bf16[2,2,256,256]{3,2,1,0:T(8,128)(2,1)}, u32[]{:S(2)}, u32[]{:S(2)}) collective-permute-start(bf16[2,2,256,256]{3,2,1,0:T(8,128)(2,1)S(1)} %get-tuple-element.16), channel_id=1, source_target_pairs={{0,65},{1,448},{2,67},{3,450},{4,69},{5,452},{6,71},{7,454},{8,73}... | collective-permute-start | bytes 1572872 | tf_op jit(solution)/shard_map/ppermute | solution.py:33
  85.5 3.4 %collective-permute-start.10 = (bf16[2,2,256,256]{3,2,1,0:T(8,128)(2,1)S(1)}, bf16[2,2,256,256]{3,2,1,0:T(8,128)(2,1)}, u32[]{:S(2)}, u32[]{:S(2)}) collective-permute-start(bf16[2,2,256,256]{3,2,1,0:T(8,128)(2,1)S(1)} %get-tuple-element.17), channel_id=1, source_target_pairs={{0,73},{1,440},{2,75},{3,442},{4,77},{5,444},{6,79},{7,446},{8,81}... | collective-permute-start | bytes 1572872 | tf_op jit(solution)/shard_map/ppermute | solution.py:33
  89.0 0.7 broadcast_in_dim.6
  89.7 6.2 %all-to-all-start = ((f32[8,32,256]{2,1,0:T(8,128)}), f32[8,32,256]{2,1,0:T(8,128)S(1)}, u32[]{:S(2)}, u32[]{:S(2)}) async-start(f32[8,32,256]{2,1,0:T(8,128)} %broadcast_in_dim.6), calls=%async_computation | async-start | bytes 524288 | tf_op jit(solution)/shard_map/all_to_all | solution.py:188
  95.9 0.0 collective-permute-done.8
  95.9 6.5 %collective-permute-done.9 = bf16[2,2,256,256]{3,2,1,0:T(8,128)(2,1)} collective-permute-done((bf16[2,2,256,256]{3,2,1,0:T(8,128)(2,1)S(1)}, bf16[2,2,256,256]{3,2,1,0:T(8,128)(2,1)}, u32[]{:S(2)}, u32[]{:S(2)}) %collective-permute-start.9) | collective-permute-done | bytes 524320 | tf_op jit(solution)/shard_map/ppermute | solution.py:33
  102.4 0.7 collective-permute-done.10
  103.1 1.6 %fusion = (bf16[2,256,256]{2,1,0:T(8,128)(2,1)S(1)}, bf16[2,256,256]{2,1,0:T(8,128)(2,1)S(1)}) fusion(bf16[2,2,256,256]{3,2,1,0:T(8,128)(2,1)} %collective-permute-done.10, bf16[2,2,256,256]{3,2,1,0:T(8,128)(2,1)} %collective-permute-done.9, bf16[2,2,256,256]{3,2,1,0:T(8,128)(2,1)} %collective-permute-done.8, bf16[2,2,256,256]{3,2,1,0:T(8,128)(2,1)S(1)} %get-tuple-element.14), kind=kLoop, calls=%fused_computation.2 | loop fusion | flops 2097152 | bytes 2621440 | tf_op jit(solution)/shard_map/add | solution.py:182
  104.7 5.3 %collective-permute-start.11 = (bf16[2,256,256]{2,1,0:T(8,128)(2,1)S(1)}, bf16[2,256,256]{2,1,0:T(8,128)(2,1)S(1)}, u32[]{:S(2)}, u32[]{:S(2)}) collective-permute-start(bf16[2,256,256]{2,1,0:T(8,128)(2,1)S(1)} %get-tuple-element.21), channel_id=1, source_target_pairs={{0,0},{1,393},{2,386},{3,267},{4,260},{5,141},{6,134},{7,15},{8,8}... | collective-permute-start | bytes 786440 | tf_op jit(solution)/shard_map/ppermute | solution.py:33
  110.0 1.9 %collective-permute-start.12 = (bf16[2,256,256]{2,1,0:T(8,128)(2,1)S(1)}, bf16[2,256,256]{2,1,0:T(8,128)(2,1)S(1)}, u32[]{:S(2)}, u32[]{:S(2)}) collective-permute-start(bf16[2,256,256]{2,1,0:T(8,128)(2,1)S(1)} %get-tuple-element.22), channel_id=1, source_target_pairs={{0,496},{1,409},{2,370},{3,283},{4,244},{5,157},{6,118},{7,31},{8,... | collective-permute-start | bytes 786440 | tf_op jit(solution)/shard_map/ppermute | solution.py:33
  112.0 0.7 slice.100
  112.7 0.0 all-to-all-done
  112.7 0.7 broadcast_in_dim.7
  113.4 3.5 %all-to-all-start.1 = ((f32[8,32,256]{2,1,0:T(8,128)}), f32[8,32,256]{2,1,0:T(8,128)S(1)}, u32[]{:S(2)}, u32[]{:S(2)}) async-start(f32[8,32,256]{2,1,0:T(8,128)} %broadcast_in_dim.7), calls=%async_computation.1 | async-start | bytes 524288 | tf_op jit(solution)/shard_map/all_to_all | solution.py:188
  117.0 0.0 collective-permute-done.11
  117.0 9.7 %collective-permute-done.12 = bf16[2,256,256]{2,1,0:T(8,128)(2,1)S(1)} collective-permute-done((bf16[2,256,256]{2,1,0:T(8,128)(2,1)S(1)}, bf16[2,256,256]{2,1,0:T(8,128)(2,1)S(1)}, u32[]{:S(2)}, u32[]{:S(2)}) %collective-permute-start.12) | collective-permute-done | bytes 262176 | tf_op jit(solution)/shard_map/ppermute | solution.py:33
  126.7 0.1 add_convert_fusion.3
  126.7 2.0 %all_gather.40 = bf16[2,256,256]{2,1,0:T(8,128)(2,1)S(1)} all-gather(bf16[1,256,256]{2,1,0:T(8,128)(2,1)S(1)} %add_convert_fusion.3), channel_id=1, replica_groups=mesh['zl'=2,'x'=4,'y'=8,'zh'=4,'c'=2] {'c'}, dimensions={0}, use_global_device_ids=true | all-gather | bytes 393216 | tf_op jit(solution)/shard_map/all_gather | solution.py:259
  128.7 0.1 fusion.3
  128.8 0.0 all-to-all-done.1
  128.9 18.5 %all-gather.3 = bf16[1152,256]{1,0:T(8,128)(2,1)S(1)} all-gather(bf16[288,256]{1,0:T(8,128)(2,1)S(1)} %pad_maximum_fusion), channel_id=5, replica_groups=mesh['zl'=2,'x'=4,'y'=8,'zh'=4,'c'=2] {'zh'}, dimensions={0}, use_global_device_ids=true | all-gather | bytes 737280 | tf_op jit(solution)/shard_map/all_gather | solution.py:261
  147.4 0.1 shard_map.80
  147.6 2.8 %all-gather.4 = bf16[768,256]{1,0:T(8,128)(2,1)S(1)} all-gather(bf16[384,256]{1,0:T(8,128)(2,1)S(1)} %shard_map.80), channel_id=6, replica_groups=mesh['zl'=2,'x'=4,'y'=8,'zh'=4,'c'=2] {'c'}, dimensions={0}, use_global_device_ids=true | all-gather | bytes 589824 | tf_op jit(solution)/shard_map/all_gather | solution.py:275
  150.4 0.8 shard_map.81
  (9 shorter events, 0.2 us)
Async XLA Ops:
  0.6 36.6 %copy-start = (bf16[512,256]{1,0:T(8,128)(2,1)S(1)}, bf16[512,256]{1,0:T(8,128)(2,1)}, u32[]{:S(2)}) copy-start(bf16[512,256]{1,0:T(8,128)(2,1)} %param.7) | copy-start | bytes 786436
  0.6 13.1 %collective-permute-start = (bf16[512,256]{1,0:T(8,128)(2,1)}, bf16[512,256]{1,0:T(8,128)(2,1)S(1)}, u32[]{:S(2)}, u32[]{:S(2)}) collective-permute-start(bf16[512,256]{1,0:T(8,128)(2,1)} %param.5), channel_id=1, source_target_pairs={{0,0},{1,121},{2,130},{3,251},{4,260},{5,381},{6,390},{7,511},{8,8... | collective-permute-start | bytes 786440 | tf_op jit(solution)/shard_map/ppermute | solution.py:33
  7.6 19.2 %collective-permute-start.4 = (bf16[512,256]{1,0:T(8,128)(2,1)}, bf16[512,256]{1,0:T(8,128)(2,1)S(1)}, u32[]{:S(2)}, u32[]{:S(2)}) collective-permute-start(bf16[512,256]{1,0:T(8,128)(2,1)} %param.5), channel_id=1, source_target_pairs={{0,16},{1,105},{2,146},{3,235},{4,276},{5,365},{6,406},{7,495},{8,... | collective-permute-start | bytes 786440 | tf_op jit(solution)/shard_map/ppermute | solution.py:33
  13.8 18.3 %collective-permute-start.3 = (bf16[512,256]{1,0:T(8,128)(2,1)S(1)}, bf16[512,256]{1,0:T(8,128)(2,1)S(1)}, u32[]{:S(2)}, u32[]{:S(2)}) collective-permute-start(bf16[512,256]{1,0:T(8,128)(2,1)S(1)} %collective-permute-done.near), channel_id=1, source_target_pairs={{0,8},{1,505},{2,10},{3,507},{4,12},{5,509},{6,14},{7,511},{8,16},... | collective-permute-start | bytes 786440 | tf_op jit(solution)/shard_map/ppermute | solution.py:33
  20.1 17.1 %collective-permute-start.2 = (bf16[512,256]{1,0:T(8,128)(2,1)S(1)}, bf16[512,256]{1,0:T(8,128)(2,1)S(1)}, u32[]{:S(2)}, u32[]{:S(2)}) collective-permute-start(bf16[512,256]{1,0:T(8,128)(2,1)S(1)} %collective-permute-done.near), channel_id=1, source_target_pairs={{0,65},{1,448},{2,67},{3,450},{4,69},{5,452},{6,71},{7,454},{8,73}... | collective-permute-start | bytes 786440 | tf_op jit(solution)/shard_map/ppermute | solution.py:33
  22.1 15.2 %collective-permute-start.1 = (bf16[512,256]{1,0:T(8,128)(2,1)S(1)}, bf16[512,256]{1,0:T(8,128)(2,1)S(1)}, u32[]{:S(2)}, u32[]{:S(2)}) collective-permute-start(bf16[512,256]{1,0:T(8,128)(2,1)S(1)} %collective-permute-done.near), channel_id=1, source_target_pairs={{0,73},{1,440},{2,75},{3,442},{4,77},{5,444},{6,79},{7,446},{8,81}... | collective-permute-start | bytes 786440 | tf_op jit(solution)/shard_map/ppermute | solution.py:33
  26.8 11.8 %collective-permute-start.7 = (bf16[512,256]{1,0:T(8,128)(2,1)S(1)}, bf16[512,256]{1,0:T(8,128)(2,1)S(1)}, u32[]{:S(2)}, u32[]{:S(2)}) collective-permute-start(bf16[512,256]{1,0:T(8,128)(2,1)S(1)} %collective-permute-done.4.far), channel_id=1, source_target_pairs={{0,8},{1,505},{2,10},{3,507},{4,12},{5,509},{6,14},{7,511},{8,16},... | collective-permute-start | bytes 786440 | tf_op jit(solution)/shard_map/ppermute | solution.py:33
  30.2 12.2 %collective-permute-start.6 = (bf16[512,256]{1,0:T(8,128)(2,1)S(1)}, bf16[512,256]{1,0:T(8,128)(2,1)S(1)}, u32[]{:S(2)}, u32[]{:S(2)}) collective-permute-start(bf16[512,256]{1,0:T(8,128)(2,1)S(1)} %collective-permute-done.4.far), channel_id=1, source_target_pairs={{0,65},{1,448},{2,67},{3,450},{4,69},{5,452},{6,71},{7,454},{8,73}... | collective-permute-start | bytes 786440 | tf_op jit(solution)/shard_map/ppermute | solution.py:33
  32.1 12.6 %collective-permute-start.5 = (bf16[512,256]{1,0:T(8,128)(2,1)S(1)}, bf16[512,256]{1,0:T(8,128)(2,1)S(1)}, u32[]{:S(2)}, u32[]{:S(2)}) collective-permute-start(bf16[512,256]{1,0:T(8,128)(2,1)S(1)} %collective-permute-done.4.far), channel_id=1, source_target_pairs={{0,73},{1,440},{2,75},{3,442},{4,77},{5,444},{6,79},{7,446},{8,81}... | collective-permute-start | bytes 786440 | tf_op jit(solution)/shard_map/ppermute | solution.py:33
  37.3 0.7 copy-start.2
  38.6 33.1 %copy-start.1 = (bf16[256,256]{1,0:T(8,128)(2,1)S(1)}, bf16[256,256]{1,0:T(8,128)(2,1)}, u32[]{:S(2)}) copy-start(bf16[256,256]{1,0:T(8,128)(2,1)} %weight_ref.1) | copy-start | bytes 393220
  38.6 36.5 %copy-start.3 = (s32[1,8]{1,0:T(1,128)S(1)}, s32[1,8]{1,0:T(1,128)}, u32[]{:S(2)}) copy-start(s32[1,8]{1,0:T(1,128)} %mask_ref.5) | copy-start | bytes 100
  76.0 19.9 %collective-permute-start.8 = (bf16[2,2,256,256]{3,2,1,0:T(8,128)(2,1)S(1)}, bf16[2,2,256,256]{3,2,1,0:T(8,128)(2,1)}, u32[]{:S(2)}, u32[]{:S(2)}) collective-permute-start(bf16[2,2,256,256]{3,2,1,0:T(8,128)(2,1)S(1)} %get-tuple-element.15), channel_id=1, source_target_pairs={{0,504},{1,9},{2,506},{3,11},{4,508},{5,13},{6,510},{7,15},{8,0},{... | collective-permute-start | bytes 1572872 | tf_op jit(solution)/shard_map/ppermute | solution.py:33
  77.9 24.5 %collective-permute-start.9 = (bf16[2,2,256,256]{3,2,1,0:T(8,128)(2,1)S(1)}, bf16[2,2,256,256]{3,2,1,0:T(8,128)(2,1)}, u32[]{:S(2)}, u32[]{:S(2)}) collective-permute-start(bf16[2,2,256,256]{3,2,1,0:T(8,128)(2,1)S(1)} %get-tuple-element.16), channel_id=1, source_target_pairs={{0,65},{1,448},{2,67},{3,450},{4,69},{5,452},{6,71},{7,454},{8,73}... | collective-permute-start | bytes 1572872 | tf_op jit(solution)/shard_map/ppermute | solution.py:33
  85.5 17.6 %collective-permute-start.10 = (bf16[2,2,256,256]{3,2,1,0:T(8,128)(2,1)S(1)}, bf16[2,2,256,256]{3,2,1,0:T(8,128)(2,1)}, u32[]{:S(2)}, u32[]{:S(2)}) collective-permute-start(bf16[2,2,256,256]{3,2,1,0:T(8,128)(2,1)S(1)} %get-tuple-element.17), channel_id=1, source_target_pairs={{0,73},{1,440},{2,75},{3,442},{4,77},{5,444},{6,79},{7,446},{8,81}... | collective-permute-start | bytes 1572872 | tf_op jit(solution)/shard_map/ppermute | solution.py:33
  89.7 23.0 %all-to-all-start = ((f32[8,32,256]{2,1,0:T(8,128)}), f32[8,32,256]{2,1,0:T(8,128)S(1)}, u32[]{:S(2)}, u32[]{:S(2)}) async-start(f32[8,32,256]{2,1,0:T(8,128)} %broadcast_in_dim.6), calls=%async_computation | async-start | bytes 524288 | tf_op jit(solution)/shard_map/all_to_all | solution.py:188
  104.7 12.3 %collective-permute-start.11 = (bf16[2,256,256]{2,1,0:T(8,128)(2,1)S(1)}, bf16[2,256,256]{2,1,0:T(8,128)(2,1)S(1)}, u32[]{:S(2)}, u32[]{:S(2)}) collective-permute-start(bf16[2,256,256]{2,1,0:T(8,128)(2,1)S(1)} %get-tuple-element.21), channel_id=1, source_target_pairs={{0,0},{1,393},{2,386},{3,267},{4,260},{5,141},{6,134},{7,15},{8,8}... | collective-permute-start | bytes 786440 | tf_op jit(solution)/shard_map/ppermute | solution.py:33
  110.0 16.6 %collective-permute-start.12 = (bf16[2,256,256]{2,1,0:T(8,128)(2,1)S(1)}, bf16[2,256,256]{2,1,0:T(8,128)(2,1)S(1)}, u32[]{:S(2)}, u32[]{:S(2)}) collective-permute-start(bf16[2,256,256]{2,1,0:T(8,128)(2,1)S(1)} %get-tuple-element.22), channel_id=1, source_target_pairs={{0,496},{1,409},{2,370},{3,283},{4,244},{5,157},{6,118},{7,31},{8,... | collective-permute-start | bytes 786440 | tf_op jit(solution)/shard_map/ppermute | solution.py:33
  113.4 15.4 %all-to-all-start.1 = ((f32[8,32,256]{2,1,0:T(8,128)}), f32[8,32,256]{2,1,0:T(8,128)S(1)}, u32[]{:S(2)}, u32[]{:S(2)}) async-start(f32[8,32,256]{2,1,0:T(8,128)} %broadcast_in_dim.7), calls=%async_computation.1 | async-start | bytes 524288 | tf_op jit(solution)/shard_map/all_to_all | solution.py:188

commit v4 on v3

--- a/solution.py
+++ b/solution.py
@@ -125,9 +125,7 @@
     pack_ref[HALF : 2 * HALF] = turned.astype(BF16)
     full[...] = lax.dot_general(high, score, (((0,), (0,)), ((), ())), preferred_element_type=F32)
     term = full[pl.ds(pl.multiple_of(zh_ref[0] * 64, 64), 64), :]
-    term_high = term.astype(BF16)
-    pack_ref[512:576] = term_high
-    pack_ref[576:640] = (term - term_high.astype(F32)).astype(BF16)
+    pack_ref[512:576] = term.astype(BF16)
 
 
 def backward_kernel(plan, core_ref, mask_ref, tiles_ref, pack_ref, *rest):
@@ -228,7 +226,7 @@
     grad_half = lax.dynamic_slice_in_dim(grad_out, core_index * HALF, HALF, 0)
     pack = pl.pallas_call(
         middle_kernel,
-        out_shape=jax.ShapeDtypeStruct((640, HIDDEN), BF16),
+        out_shape=jax.ShapeDtypeStruct((576, HIDDEN), BF16),
         in_specs=[SMEM] + [VMEM] * 3,
         out_specs=VMEM,
         scratch_shapes=[pltpu.VMEM((HIDDEN, HIDDEN), F32)],
@@ -246,8 +244,8 @@
     home_near = route(near, lambda i, r: (i - 8 * r - 7 * (r % 2), r))
     home_far = route(far, lambda i, r: (i - 8 * r - 2 - 3 * (r % 2), r))
 
-    high, low = packs[:, 512:576].astype(F32), packs[:, 576:640].astype(F32)
-    term = lax.dynamic_slice_in_dim(high[0] + low[0] + (high[1] + low[1]), core_index * 32, 32, 0)
+    terms = packs[:, 512:576].astype(F32)
+    term = lax.dynamic_slice_in_dim(terms[0] + terms[1], core_index * 32, 32, 0)
     term = spread_sum(term, "y")
     term, _ = lax.optimization_barrier((term, far))
     term = (spread_sum(term, ("zl", "x")) * (BLOCKS * ROWS) ** -0.5).astype(BF16)

time: 151 us -> 150 us (level)
  blocking collectives: 52.4 us -> 55.6 us
  starting transfers between devices: 66.3 us -> 63.2 us
    all_gather x1, blocking collectives: 18.5 us -> 21.7 us  [shards(): grad_parts = lax.all_gather(jnp.concatenate([chip_grad, term]), 'zh')]
    ppermute x13, starting transfers between devices: 56.6 us -> 53.5 us  [route(): return lax.ppermute(value, AXES, pairs)]
    ppermute x13, waiting for transfers between devices: 23.1 us -> 21.6 us  [route(): return lax.ppermute(value, AXES, pairs)]
  transfers between devices with their start and end apart: 15 -> 15, of which waited for: 5 -> 6; matrix products, arithmetic and copies ran while one was open for 3% -> 3% of each run, Pallas kernels for 0% -> 0%
where the time goes in v4:
time: 150 us; the launch traced here: 151 us
  starting transfers between devices  63.2 us (42%)
  blocking collectives  55.6 us (37%)
  waiting for transfers between devices  22.6 us (15%)
  Pallas kernels  3.69 us (2%)
  local copies, waits for them, and re-layouts  2.87 us (2%)
  other arithmetic  1.9 us (1%)
    ppermute x13, starting transfers between devices, route(): return lax.ppermute(value, AXES, pairs)  53.5 us
    all_gather x1, blocking collectives, shards(): parts = lax.all_gather(chip, 'zh')  22.5 us
    all_gather x1, blocking collectives, shards(): grad_parts = lax.all_gather(jnp.concatenate([chip_grad, term]), 'zh')  21.7 us
    ppermute x13, waiting for transfers between devices, route(): return lax.ppermute(value, AXES, pairs)  21.6 us
    all_to_all x2, starting transfers between devices, spread_sum(): return jnp.sum(lax.all_to_all(copies, axes, 0, 0), axis=0)  9.66 us
    all_gather x1, blocking collectives, shards(): packs = lax.all_gather(pack, 'c')  3.62 us
    all_gather x1, blocking collectives, shards(): sent = lax.all_gather(send, 'c')  3.07 us
  transfers between devices with their start and end apart: 15, of which 6 were waited for; matrix products, arithmetic and copies ran while one was open for 3% of the time, Pallas kernels for 0%

profile of v4, /device:TPU:1, one launch (start us, length us, event | category | flops | bytes accessed | tf_op | source)
XLA Modules:
  0.0 150.9 jit_solution(3740739756575346465)
XLA Ops:
  0.6 0.0 copy-start
  0.6 7.0 %collective-permute-start = (bf16[512,256]{1,0:T(8,128)(2,1)}, bf16[512,256]{1,0:T(8,128)(2,1)S(1)}, u32[]{:S(2)}, u32[]{:S(2)}) collective-permute-start(bf16[512,256]{1,0:T(8,128)(2,1)} %param.5), channel_id=1, source_target_pairs={{0,0},{1,121},{2,130},{3,251},{4,260},{5,381},{6,390},{7,511},{8,8... | collective-permute-start | bytes 786440 | tf_op jit(solution)/shard_map/ppermute | solution.py:33
  7.6 6.1 %collective-permute-start.4 = (bf16[512,256]{1,0:T(8,128)(2,1)}, bf16[512,256]{1,0:T(8,128)(2,1)S(1)}, u32[]{:S(2)}, u32[]{:S(2)}) collective-permute-start(bf16[512,256]{1,0:T(8,128)(2,1)} %param.5), channel_id=1, source_target_pairs={{0,16},{1,105},{2,146},{3,235},{4,276},{5,365},{6,406},{7,495},{8,... | collective-permute-start | bytes 786440 | tf_op jit(solution)/shard_map/ppermute | solution.py:33
  13.8 0.0 collective-permute-done.near
  13.8 6.4 %collective-permute-start.3 = (bf16[512,256]{1,0:T(8,128)(2,1)S(1)}, bf16[512,256]{1,0:T(8,128)(2,1)S(1)}, u32[]{:S(2)}, u32[]{:S(2)}) collective-permute-start(bf16[512,256]{1,0:T(8,128)(2,1)S(1)} %collective-permute-done.near), channel_id=1, source_target_pairs={{0,8},{1,505},{2,10},{3,507},{4,12},{5,509},{6,14},{7,511},{8,16},... | collective-permute-start | bytes 786440 | tf_op jit(solution)/shard_map/ppermute | solution.py:33
  20.1 1.9 %collective-permute-start.2 = (bf16[512,256]{1,0:T(8,128)(2,1)S(1)}, bf16[512,256]{1,0:T(8,128)(2,1)S(1)}, u32[]{:S(2)}, u32[]{:S(2)}) collective-permute-start(bf16[512,256]{1,0:T(8,128)(2,1)S(1)} %collective-permute-done.near), channel_id=1, source_target_pairs={{0,65},{1,448},{2,67},{3,450},{4,69},{5,452},{6,71},{7,454},{8,73}... | collective-permute-start | bytes 786440 | tf_op jit(solution)/shard_map/ppermute | solution.py:33
  22.1 4.7 %collective-permute-start.1 = (bf16[512,256]{1,0:T(8,128)(2,1)S(1)}, bf16[512,256]{1,0:T(8,128)(2,1)S(1)}, u32[]{:S(2)}, u32[]{:S(2)}) collective-permute-start(bf16[512,256]{1,0:T(8,128)(2,1)S(1)} %collective-permute-done.near), channel_id=1, source_target_pairs={{0,73},{1,440},{2,75},{3,442},{4,77},{5,444},{6,79},{7,446},{8,81}... | collective-permute-start | bytes 786440 | tf_op jit(solution)/shard_map/ppermute | solution.py:33
  26.8 0.0 collective-permute-done.4.far
  26.8 3.4 %collective-permute-start.7 = (bf16[512,256]{1,0:T(8,128)(2,1)S(1)}, bf16[512,256]{1,0:T(8,128)(2,1)S(1)}, u32[]{:S(2)}, u32[]{:S(2)}) collective-permute-start(bf16[512,256]{1,0:T(8,128)(2,1)S(1)} %collective-permute-done.4.far), channel_id=1, source_target_pairs={{0,8},{1,505},{2,10},{3,507},{4,12},{5,509},{6,14},{7,511},{8,16},... | collective-permute-start | bytes 786440 | tf_op jit(solution)/shard_map/ppermute | solution.py:33
  30.2 1.9 %collective-permute-start.6 = (bf16[512,256]{1,0:T(8,128)(2,1)S(1)}, bf16[512,256]{1,0:T(8,128)(2,1)S(1)}, u32[]{:S(2)}, u32[]{:S(2)}) collective-permute-start(bf16[512,256]{1,0:T(8,128)(2,1)S(1)} %collective-permute-done.4.far), channel_id=1, source_target_pairs={{0,65},{1,448},{2,67},{3,450},{4,69},{5,452},{6,71},{7,454},{8,73}... | collective-permute-start | bytes 786440 | tf_op jit(solution)/shard_map/ppermute | solution.py:33
  32.1 0.0 collective-permute-done.3.near_r
  32.1 5.1 %collective-permute-start.5 = (bf16[512,256]{1,0:T(8,128)(2,1)S(1)}, bf16[512,256]{1,0:T(8,128)(2,1)S(1)}, u32[]{:S(2)}, u32[]{:S(2)}) collective-permute-start(bf16[512,256]{1,0:T(8,128)(2,1)S(1)} %collective-permute-done.4.far), channel_id=1, source_target_pairs={{0,73},{1,440},{2,75},{3,442},{4,77},{5,444},{6,79},{7,446},{8,81}... | collective-permute-start | bytes 786440 | tf_op jit(solution)/shard_map/ppermute | solution.py:33
  37.2 0.0 copy-done
  37.2 0.0 collective-permute-done.2.near_e
  37.2 0.0 collective-permute-done.1.near_d
  37.3 0.0 copy-start.2
  37.3 0.6 copy-done.2
  37.9 0.7 shard_map.76.before
  38.6 0.0 copy-start.1
  38.6 0.0 copy-start.3
  38.6 0.0 collective-permute-done.7.far_r
  38.6 3.8 %collective-permute-done.6.far_e = bf16[512,256]{1,0:T(8,128)(2,1)S(1)} collective-permute-done((bf16[512,256]{1,0:T(8,128)(2,1)S(1)}, bf16[512,256]{1,0:T(8,128)(2,1)S(1)}, u32[]{:S(2)}, u32[]{:S(2)}) %collective-permute-start.6) | collective-permute-done | bytes 262176 | tf_op jit(solution)/shard_map/ppermute | solution.py:33
  42.4 2.4 %collective-permute-done.5.far_d = bf16[512,256]{1,0:T(8,128)(2,1)S(1)} collective-permute-done((bf16[512,256]{1,0:T(8,128)(2,1)S(1)}, bf16[512,256]{1,0:T(8,128)(2,1)S(1)}, u32[]{:S(2)}, u32[]{:S(2)}) %collective-permute-start.5) | collective-permute-done | bytes 262176 | tf_op jit(solution)/shard_map/ppermute | solution.py:33
  44.8 0.7 shard_map.77
  45.4 3.1 %all-gather = bf16[512,256]{1,0:T(8,128)(2,1)S(1)} all-gather(bf16[256,256]{1,0:T(8,128)(2,1)S(1)} %get-tuple-element.13), channel_id=2, replica_groups=mesh['zl'=2,'x'=4,'y'=8,'zh'=4,'c'=2] {'c'}, dimensions={0}, use_global_device_ids=true | all-gather | bytes 393216 | tf_op jit(solution)/shard_map/all_gather | solution.py:223
  48.5 22.5 %all-gather.1 = bf16[1024,256]{1,0:T(8,128)(2,1)S(1)} all-gather(bf16[256,256]{1,0:T(8,128)(2,1)S(1)} %fusion.2), channel_id=3, replica_groups=mesh['zl'=2,'x'=4,'y'=8,'zh'=4,'c'=2] {'zh'}, dimensions={0}, use_global_device_ids=true | all-gather | bytes 655360 | tf_op jit(solution)/shard_map/all_gather | solution.py:225
  71.1 0.0 copy-done.1
  71.1 0.6 shard_map.78
  71.7 3.6 %all-gather.2 = bf16[1152,256]{1,0:T(8,128)(2,1)S(1)} all-gather(bf16[576,256]{1,0:T(8,128)(2,1)S(1)} %shard_map.78), channel_id=4, replica_groups=mesh['zl'=2,'x'=4,'y'=8,'zh'=4,'c'=2] {'c'}, dimensions={0}, use_global_device_ids=true | all-gather | bytes 884736 | tf_op jit(solution)/shard_map/all_gather | solution.py:235
  75.3 0.0 copy-done.3
  75.3 0.9 shard_map.79
  76.2 4.1 %collective-permute-start.8 = (bf16[2,2,256,256]{3,2,1,0:T(8,128)(2,1)S(1)}, bf16[2,2,256,256]{3,2,1,0:T(8,128)(2,1)}, u32[]{:S(2)}, u32[]{:S(2)}) collective-permute-start(bf16[2,2,256,256]{3,2,1,0:T(8,128)(2,1)S(1)} %get-tuple-element.15), channel_id=1, source_target_pairs={{0,504},{1,9},{2,506},{3,11},{4,508},{5,13},{6,510},{7,15},{8,0},{... | collective-permute-start | bytes 1572872 | tf_op jit(solution)/shard_map/ppermute | solution.py:33
  80.3 5.1 %collective-permute-start.9 = (bf16[2,2,256,256]{3,2,1,0:T(8,128)(2,1)S(1)}, bf16[2,2,256,256]{3,2,1,0:T(8,128)(2,1)}, u32[]{:S(2)}, u32[]{:S(2)}) collective-permute-start(bf16[2,2,256,256]{3,2,1,0:T(8,128)(2,1)S(1)} %get-tuple-element.16), channel_id=1, source_target_pairs={{0,65},{1,448},{2,67},{3,450},{4,69},{5,452},{6,71},{7,454},{8,73}... | collective-permute-start | bytes 1572872 | tf_op jit(solution)/shard_map/ppermute | solution.py:33
  85.4 3.7 %collective-permute-start.10 = (bf16[2,2,256,256]{3,2,1,0:T(8,128)(2,1)S(1)}, bf16[2,2,256,256]{3,2,1,0:T(8,128)(2,1)}, u32[]{:S(2)}, u32[]{:S(2)}) collective-permute-start(bf16[2,2,256,256]{3,2,1,0:T(8,128)(2,1)S(1)} %get-tuple-element.17), channel_id=1, source_target_pairs={{0,73},{1,440},{2,75},{3,442},{4,77},{5,444},{6,79},{7,446},{8,81}... | collective-permute-start | bytes 1572872 | tf_op jit(solution)/shard_map/ppermute | solution.py:33
  89.1 0.7 broadcast_in_dim.6
  89.8 4.8 %all-to-all-start = ((f32[8,32,256]{2,1,0:T(8,128)}), f32[8,32,256]{2,1,0:T(8,128)S(1)}, u32[]{:S(2)}, u32[]{:S(2)}) async-start(f32[8,32,256]{2,1,0:T(8,128)} %broadcast_in_dim.6), calls=%async_computation | async-start | bytes 524288 | tf_op jit(solution)/shard_map/all_to_all | solution.py:186
  94.7 0.0 collective-permute-done.8
  94.7 6.0 %collective-permute-done.9 = bf16[2,2,256,256]{3,2,1,0:T(8,128)(2,1)} collective-permute-done((bf16[2,2,256,256]{3,2,1,0:T(8,128)(2,1)S(1)}, bf16[2,2,256,256]{3,2,1,0:T(8,128)(2,1)}, u32[]{:S(2)}, u32[]{:S(2)}) %collective-permute-start.9) | collective-permute-done | bytes 524320 | tf_op jit(solution)/shard_map/ppermute | solution.py:33
  100.7 4.0 %collective-permute-done.10 = bf16[2,2,256,256]{3,2,1,0:T(8,128)(2,1)} collective-permute-done((bf16[2,2,256,256]{3,2,1,0:T(8,128)(2,1)S(1)}, bf16[2,2,256,256]{3,2,1,0:T(8,128)(2,1)}, u32[]{:S(2)}, u32[]{:S(2)}) %collective-permute-start.10) | collective-permute-done | bytes 524320 | tf_op jit(solution)/shard_map/ppermute | solution.py:33
  104.7 1.6 %fusion = (bf16[2,256,256]{2,1,0:T(8,128)(2,1)S(1)}, bf16[2,256,256]{2,1,0:T(8,128)(2,1)S(1)}) fusion(bf16[2,2,256,256]{3,2,1,0:T(8,128)(2,1)} %collective-permute-done.10, bf16[2,2,256,256]{3,2,1,0:T(8,128)(2,1)} %collective-permute-done.9, bf16[2,2,256,256]{3,2,1,0:T(8,128)(2,1)} %collective-permute-done.8, bf16[2,2,256,256]{3,2,1,0:T(8,128)(2,1)S(1)} %get-tuple-element.14), kind=kLoop, calls=%fused_computation.2 | loop fusion | flops 2097152 | bytes 2621440 | tf_op jit(solution)/shard_map/add | solution.py:180
  106.3 1.9 %collective-permute-start.11 = (bf16[2,256,256]{2,1,0:T(8,128)(2,1)S(1)}, bf16[2,256,256]{2,1,0:T(8,128)(2,1)S(1)}, u32[]{:S(2)}, u32[]{:S(2)}) collective-permute-start(bf16[2,256,256]{2,1,0:T(8,128)(2,1)S(1)} %get-tuple-element.21), channel_id=1, source_target_pairs={{0,0},{1,393},{2,386},{3,267},{4,260},{5,141},{6,134},{7,15},{8,8}... | collective-permute-start | bytes 786440 | tf_op jit(solution)/shard_map/ppermute | solution.py:33
  108.2 2.3 %collective-permute-start.12 = (bf16[2,256,256]{2,1,0:T(8,128)(2,1)S(1)}, bf16[2,256,256]{2,1,0:T(8,128)(2,1)S(1)}, u32[]{:S(2)}, u32[]{:S(2)}) collective-permute-start(bf16[2,256,256]{2,1,0:T(8,128)(2,1)S(1)} %get-tuple-element.22), channel_id=1, source_target_pairs={{0,496},{1,409},{2,370},{3,283},{4,244},{5,157},{6,118},{7,31},{8,... | collective-permute-start | bytes 786440 | tf_op jit(solution)/shard_map/ppermute | solution.py:33
  110.5 0.7 slice.88
  111.2 0.0 all-to-all-done
  111.3 0.7 broadcast_in_dim.7
  112.0 4.8 %all-to-all-start.1 = ((f32[8,32,256]{2,1,0:T(8,128)}), f32[8,32,256]{2,1,0:T(8,128)S(1)}, u32[]{:S(2)}, u32[]{:S(2)}) async-start(f32[8,32,256]{2,1,0:T(8,128)} %broadcast_in_dim.7), calls=%async_computation.1 | async-start | bytes 524288 | tf_op jit(solution)/shard_map/all_to_all | solution.py:186
  116.8 0.0 collective-permute-done.11
  116.8 5.4 %collective-permute-done.12 = bf16[2,256,256]{2,1,0:T(8,128)(2,1)S(1)} collective-permute-done((bf16[2,256,256]{2,1,0:T(8,128)(2,1)S(1)}, bf16[2,256,256]{2,1,0:T(8,128)(2,1)S(1)}, u32[]{:S(2)}, u32[]{:S(2)}) %collective-permute-start.12) | collective-permute-done | bytes 262176 | tf_op jit(solution)/shard_map/ppermute | solution.py:33
  122.2 0.1 add_convert_fusion.3
  122.3 2.0 %all_gather.40 = bf16[2,256,256]{2,1,0:T(8,128)(2,1)S(1)} all-gather(bf16[1,256,256]{2,1,0:T(8,128)(2,1)S(1)} %add_convert_fusion.3), channel_id=1, replica_groups=mesh['zl'=2,'x'=4,'y'=8,'zh'=4,'c'=2] {'c'}, dimensions={0}, use_global_device_ids=true | all-gather | bytes 393216 | tf_op jit(solution)/shard_map/all_gather | solution.py:257
  124.3 0.1 fusion.3
  124.4 1.0 all-to-all-done.1
  125.5 21.7 %all-gather.3 = bf16[1152,256]{1,0:T(8,128)(2,1)S(1)} all-gather(bf16[288,256]{1,0:T(8,128)(2,1)S(1)} %pad_maximum_fusion), channel_id=5, replica_groups=mesh['zl'=2,'x'=4,'y'=8,'zh'=4,'c'=2] {'zh'}, dimensions={0}, use_global_device_ids=true | all-gather | bytes 737280 | tf_op jit(solution)/shard_map/all_gather | solution.py:259
  147.1 0.1 shard_map.80
  147.3 2.8 %all-gather.4 = bf16[768,256]{1,0:T(8,128)(2,1)S(1)} all-gather(bf16[384,256]{1,0:T(8,128)(2,1)S(1)} %shard_map.80), channel_id=6, replica_groups=mesh['zl'=2,'x'=4,'y'=8,'zh'=4,'c'=2] {'c'}, dimensions={0}, use_global_device_ids=true | all-gather | bytes 589824 | tf_op jit(solution)/shard_map/all_gather | solution.py:273
  150.0 0.8 shard_map.81
  (9 shorter events, 0.2 us)
Async XLA Ops:
  0.6 36.6 %copy-start = (bf16[512,256]{1,0:T(8,128)(2,1)S(1)}, bf16[512,256]{1,0:T(8,128)(2,1)}, u32[]{:S(2)}) copy-start(bf16[512,256]{1,0:T(8,128)(2,1)} %param.7) | copy-start | bytes 786436
  0.6 13.1 %collective-permute-start = (bf16[512,256]{1,0:T(8,128)(2,1)}, bf16[512,256]{1,0:T(8,128)(2,1)S(1)}, u32[]{:S(2)}, u32[]{:S(2)}) collective-permute-start(bf16[512,256]{1,0:T(8,128)(2,1)} %param.5), channel_id=1, source_target_pairs={{0,0},{1,121},{2,130},{3,251},{4,260},{5,381},{6,390},{7,511},{8,8... | collective-permute-start | bytes 786440 | tf_op jit(solution)/shard_map/ppermute | solution.py:33
  7.6 19.2 %collective-permute-start.4 = (bf16[512,256]{1,0:T(8,128)(2,1)}, bf16[512,256]{1,0:T(8,128)(2,1)S(1)}, u32[]{:S(2)}, u32[]{:S(2)}) collective-permute-start(bf16[512,256]{1,0:T(8,128)(2,1)} %param.5), channel_id=1, source_target_pairs={{0,16},{1,105},{2,146},{3,235},{4,276},{5,365},{6,406},{7,495},{8,... | collective-permute-start | bytes 786440 | tf_op jit(solution)/shard_map/ppermute | solution.py:33
  13.8 18.3 %collective-permute-start.3 = (bf16[512,256]{1,0:T(8,128)(2,1)S(1)}, bf16[512,256]{1,0:T(8,128)(2,1)S(1)}, u32[]{:S(2)}, u32[]{:S(2)}) collective-permute-start(bf16[512,256]{1,0:T(8,128)(2,1)S(1)} %collective-permute-done.near), channel_id=1, source_target_pairs={{0,8},{1,505},{2,10},{3,507},{4,12},{5,509},{6,14},{7,511},{8,16},... | collective-permute-start | bytes 786440 | tf_op jit(solution)/shard_map/ppermute | solution.py:33
  20.1 17.1 %collective-permute-start.2 = (bf16[512,256]{1,0:T(8,128)(2,1)S(1)}, bf16[512,256]{1,0:T(8,128)(2,1)S(1)}, u32[]{:S(2)}, u32[]{:S(2)}) collective-permute-start(bf16[512,256]{1,0:T(8,128)(2,1)S(1)} %collective-permute-done.near), channel_id=1, source_target_pairs={{0,65},{1,448},{2,67},{3,450},{4,69},{5,452},{6,71},{7,454},{8,73}... | collective-permute-start | bytes 786440 | tf_op jit(solution)/shard_map/ppermute | solution.py:33
  22.1 15.2 %collective-permute-start.1 = (bf16[512,256]{1,0:T(8,128)(2,1)S(1)}, bf16[512,256]{1,0:T(8,128)(2,1)S(1)}, u32[]{:S(2)}, u32[]{:S(2)}) collective-permute-start(bf16[512,256]{1,0:T(8,128)(2,1)S(1)} %collective-permute-done.near), channel_id=1, source_target_pairs={{0,73},{1,440},{2,75},{3,442},{4,77},{5,444},{6,79},{7,446},{8,81}... | collective-permute-start | bytes 786440 | tf_op jit(solution)/shard_map/ppermute | solution.py:33
  26.8 11.8 %collective-permute-start.7 = (bf16[512,256]{1,0:T(8,128)(2,1)S(1)}, bf16[512,256]{1,0:T(8,128)(2,1)S(1)}, u32[]{:S(2)}, u32[]{:S(2)}) collective-permute-start(bf16[512,256]{1,0:T(8,128)(2,1)S(1)} %collective-permute-done.4.far), channel_id=1, source_target_pairs={{0,8},{1,505},{2,10},{3,507},{4,12},{5,509},{6,14},{7,511},{8,16},... | collective-permute-start | bytes 786440 | tf_op jit(solution)/shard_map/ppermute | solution.py:33
  30.2 12.2 %collective-permute-start.6 = (bf16[512,256]{1,0:T(8,128)(2,1)S(1)}, bf16[512,256]{1,0:T(8,128)(2,1)S(1)}, u32[]{:S(2)}, u32[]{:S(2)}) collective-permute-start(bf16[512,256]{1,0:T(8,128)(2,1)S(1)} %collective-permute-done.4.far), channel_id=1, source_target_pairs={{0,65},{1,448},{2,67},{3,450},{4,69},{5,452},{6,71},{7,454},{8,73}... | collective-permute-start | bytes 786440 | tf_op jit(solution)/shard_map/ppermute | solution.py:33
  32.1 12.6 %collective-permute-start.5 = (bf16[512,256]{1,0:T(8,128)(2,1)S(1)}, bf16[512,256]{1,0:T(8,128)(2,1)S(1)}, u32[]{:S(2)}, u32[]{:S(2)}) collective-permute-start(bf16[512,256]{1,0:T(8,128)(2,1)S(1)} %collective-permute-done.4.far), channel_id=1, source_target_pairs={{0,73},{1,440},{2,75},{3,442},{4,77},{5,444},{6,79},{7,446},{8,81}... | collective-permute-start | bytes 786440 | tf_op jit(solution)/shard_map/ppermute | solution.py:33
  37.3 0.7 copy-start.2
  38.6 32.5 %copy-start.1 = (bf16[256,256]{1,0:T(8,128)(2,1)S(1)}, bf16[256,256]{1,0:T(8,128)(2,1)}, u32[]{:S(2)}) copy-start(bf16[256,256]{1,0:T(8,128)(2,1)} %weight_ref.1) | copy-start | bytes 393220
  38.6 36.7 %copy-start.3 = (s32[1,8]{1,0:T(1,128)S(1)}, s32[1,8]{1,0:T(1,128)}, u32[]{:S(2)}) copy-start(s32[1,8]{1,0:T(1,128)} %mask_ref.5) | copy-start | bytes 100
  76.2 18.5 %collective-permute-start.8 = (bf16[2,2,256,256]{3,2,1,0:T(8,128)(2,1)S(1)}, bf16[2,2,256,256]{3,2,1,0:T(8,128)(2,1)}, u32[]{:S(2)}, u32[]{:S(2)}) collective-permute-start(bf16[2,2,256,256]{3,2,1,0:T(8,128)(2,1)S(1)} %get-tuple-element.15), channel_id=1, source_target_pairs={{0,504},{1,9},{2,506},{3,11},{4,508},{5,13},{6,510},{7,15},{8,0},{... | collective-permute-start | bytes 1572872 | tf_op jit(solution)/shard_map/ppermute | solution.py:33
  80.3 20.4 %collective-permute-start.9 = (bf16[2,2,256,256]{3,2,1,0:T(8,128)(2,1)S(1)}, bf16[2,2,256,256]{3,2,1,0:T(8,128)(2,1)}, u32[]{:S(2)}, u32[]{:S(2)}) collective-permute-start(bf16[2,2,256,256]{3,2,1,0:T(8,128)(2,1)S(1)} %get-tuple-element.16), channel_id=1, source_target_pairs={{0,65},{1,448},{2,67},{3,450},{4,69},{5,452},{6,71},{7,454},{8,73}... | collective-permute-start | bytes 1572872 | tf_op jit(solution)/shard_map/ppermute | solution.py:33
  85.4 19.3 %collective-permute-start.10 = (bf16[2,2,256,256]{3,2,1,0:T(8,128)(2,1)S(1)}, bf16[2,2,256,256]{3,2,1,0:T(8,128)(2,1)}, u32[]{:S(2)}, u32[]{:S(2)}) collective-permute-start(bf16[2,2,256,256]{3,2,1,0:T(8,128)(2,1)S(1)} %get-tuple-element.17), channel_id=1, source_target_pairs={{0,73},{1,440},{2,75},{3,442},{4,77},{5,444},{6,79},{7,446},{8,81}... | collective-permute-start | bytes 1572872 | tf_op jit(solution)/shard_map/ppermute | solution.py:33
  89.8 21.4 %all-to-all-start = ((f32[8,32,256]{2,1,0:T(8,128)}), f32[8,32,256]{2,1,0:T(8,128)S(1)}, u32[]{:S(2)}, u32[]{:S(2)}) async-start(f32[8,32,256]{2,1,0:T(8,128)} %broadcast_in_dim.6), calls=%async_computation | async-start | bytes 524288 | tf_op jit(solution)/shard_map/all_to_all | solution.py:186
  106.3 10.5 %collective-permute-start.11 = (bf16[2,256,256]{2,1,0:T(8,128)(2,1)S(1)}, bf16[2,256,256]{2,1,0:T(8,128)(2,1)S(1)}, u32[]{:S(2)}, u32[]{:S(2)}) collective-permute-start(bf16[2,256,256]{2,1,0:T(8,128)(2,1)S(1)} %get-tuple-element.21), channel_id=1, source_target_pairs={{0,0},{1,393},{2,386},{3,267},{4,260},{5,141},{6,134},{7,15},{8,8}... | collective-permute-start | bytes 786440 | tf_op jit(solution)/shard_map/ppermute | solution.py:33
  108.2 14.0 %collective-permute-start.12 = (bf16[2,256,256]{2,1,0:T(8,128)(2,1)S(1)}, bf16[2,256,256]{2,1,0:T(8,128)(2,1)S(1)}, u32[]{:S(2)}, u32[]{:S(2)}) collective-permute-start(bf16[2,256,256]{2,1,0:T(8,128)(2,1)S(1)} %get-tuple-element.22), channel_id=1, source_target_pairs={{0,496},{1,409},{2,370},{3,283},{4,244},{5,157},{6,118},{7,31},{8,... | collective-permute-start | bytes 786440 | tf_op jit(solution)/shard_map/ppermute | solution.py:33
  112.0 13.4 %all-to-all-start.1 = ((f32[8,32,256]{2,1,0:T(8,128)}), f32[8,32,256]{2,1,0:T(8,128)S(1)}, u32[]{:S(2)}, u32[]{:S(2)}) async-start(f32[8,32,256]{2,1,0:T(8,128)} %broadcast_in_dim.7), calls=%async_computation.1 | async-start | bytes 524288 | tf_op jit(solution)/shard_map/all_to_all | solution.py:186
